TPU v7x, 256 devices: a whole 4x4x8 slice. The times are simulated.
256 devices in a mesh: rec: 2 (over core), tm: 128 (over y, x, z).
Axes of the slice: x: 4, y: 4, z: 8, core: 2. Of those that a mesh axis runs over, the one named last changes fastest.
Arguments:
- frames: bfloat16 [2, 131072, 1280], P('rec', 'tm'), may hold values from -6 to 6
- segments: int32 [2, 256, 2], P('rec'), may hold values from 0 to 131072, as said below
- ln_gain: float32 [1280], replicated, may hold values from 0.5 to 6
- w_query: bfloat16 [1280, 640], replicated, may hold values from -0.15625 to 0.15625
- w_key: bfloat16 [1280, 640], replicated, may hold values from -0.15625 to 0.15625
- w_value: bfloat16 [1280, 640], replicated, may hold values from -0.15625 to 0.15625
- w_out: bfloat16 [640, 1280], replicated, may hold values from -0.25 to 0.25
- conv_gain: float32 [1280], replicated, may hold values from 0.5 to 1.5
- conv_weight: float32 [31, 1280], replicated, may hold values from -1 to 1
Outputs:
- layer_out: bfloat16 [2, 131072, 1280], P('rec', 'tm')
Inputs may be any that keep to these rules, and one draw needn't show every extreme that they name: `segments`: per recording, 256 pairs [start, end) of multiples of 128, increasing, with 128 or more frames between one end and the next start; the first starts at 0, the last ends at 131072, half of the frames lie inside pairs, and one pair covers frames 131072 // 2 - 1024 to 65536.
All inputs are finite; a program needn't handle non-finite values.
Results may differ from a plain program's by a relative error of at most 0.0059.
The roundings to bfloat16 on the way count: a program that leaves them out, or rounds other values in their place, can miss the bound.
Values may be sent and summed in bfloat16 or wider, within the bound.
No kernel may reach another device: no remote copies, remote signals or barrier semaphores. Data moves between devices by JAX's collectives and lax.ppermute only.
A program may use at most 128 MiB of HBM per device.

v0:
```python
import jax
import jax.numpy as jnp
from jax import lax
from jax.sharding import PartitionSpec as P

H = 10
HS = 64
CTX = 256
KSZ = 31


def shifted(shard, axis, by):
    peers = lax.axis_size(axis)
    pairs = [(i, i + by) for i in range(peers) if 0 <= i + by < peers]
    return lax.ppermute(shard, axis, pairs)


def from_partner(value, axis, distance):
    mask = 2**distance
    pairs = [(source, source ^ mask) for source in range(lax.axis_size(axis))]
    return lax.ppermute(value, axis, pairs)


def normalize(values, gain):
    mean = jnp.mean(values, axis=-1, keepdims=True)
    centred = values - mean
    var = jnp.mean(centred * centred, axis=-1, keepdims=True)
    return centred * lax.rsqrt(var + 1e-05) * gain


def speech_mask(times, segs):
    inside = (times[:, None] >= segs[None, :, 0]) & (times[:, None] < segs[None, :, 1])
    return jnp.any(inside, axis=1)


def per_device(frames, segments, ln_gain, w_query, w_key, w_value, w_out, conv_gain, conv_weight):
    x = frames[0]
    segs = segments[0]
    count_rows, width = x.shape
    feats = H * HS
    query_rows = 128
    span_rows = query_rows + CTX
    reach = CTX // query_rows
    block_count = count_rows // query_rows
    half_count = block_count // 2
    group_size = max(1, min(512, count_rows) // query_rows)
    top_bit = lax.axis_size("tm").bit_length() - 2
    base = lax.axis_index("tm") * count_rows
    own_times = base + jnp.arange(count_rows, dtype=jnp.int32)
    speech = speech_mask(own_times, segs)
    normed = normalize(x.astype(jnp.float32), ln_gain).astype(jnp.bfloat16)
    tail = shifted(normed[count_rows - CTX :], "tm", 1)
    normed_ext = jnp.concatenate([tail, normed], axis=0)
    pieces = normed_ext.reshape(block_count + reach, query_rows, width)
    windows = jnp.concatenate(
        [pieces[step : step + block_count] for step in range(reach + 1)], axis=1
    )
    busy = jnp.any(speech.reshape(block_count, query_rows), axis=1).astype(jnp.int32)
    rank = jnp.cumsum(busy) - 1
    slot_ids = jnp.arange(block_count, dtype=jnp.int32)
    select = (busy[None, :] == 1) & (rank[None, :] == slot_ids[:, None])
    slot_block = jnp.sum(jnp.where(select, slot_ids[None, :], 0), axis=1)
    n_busy = jnp.sum(busy)
    own_windows = jnp.take(windows, slot_block, axis=0)
    own_starts = base + slot_block * query_rows
    send_count = n_busy // 2
    keep = n_busy - send_count
    outgoing = jnp.clip(keep + jnp.arange(half_count, dtype=jnp.int32), 0, block_count - 1)
    send_rows = jnp.take(own_windows, outgoing, axis=0)
    send_starts = jnp.take(own_starts, outgoing, axis=0)
    got_rows, got_starts, got_count = from_partner(
        (send_rows, send_starts, send_count.reshape(1)), "tm", top_bit
    )
    mine = slot_ids < keep
    from_got = jnp.clip(slot_ids - keep, 0, half_count - 1)
    work_rows = jnp.where(mine[:, None, None], own_windows, jnp.take(got_rows, from_got, axis=0))
    work_starts = jnp.where(mine, own_starts, jnp.take(got_starts, from_got, axis=0))
    total_slots = work_rows.shape[0]
    groups = (keep + got_count[0] + group_size - 1) // group_size
    empty = jnp.zeros((total_slots, query_rows, feats), jnp.bfloat16)

    def one_group(index, result):
        first = index * group_size
        rows = lax.dynamic_slice_in_dim(work_rows, first, group_size, 0)
        begin = lax.dynamic_slice_in_dim(work_starts, first, group_size, 0)
        flat = rows.reshape(group_size * span_rows, width)
        keys = jnp.dot(flat, w_key, preferred_element_type=jnp.float32).astype(jnp.bfloat16)
        values = jnp.dot(flat, w_value, preferred_element_type=jnp.float32).astype(jnp.bfloat16)
        asking = rows[:, CTX:].reshape(group_size * query_rows, width)
        queries = jnp.dot(asking, w_query, preferred_element_type=jnp.float32).astype(jnp.bfloat16)
        keys = keys.reshape(group_size, span_rows, H, HS)
        values = values.reshape(group_size, span_rows, H, HS)
        queries = queries.reshape(group_size, query_rows, H, HS)
        tq = begin[:, None] + jnp.arange(query_rows, dtype=jnp.int32)[None, :]
        tk = begin[:, None] - CTX + jnp.arange(span_rows, dtype=jnp.int32)[None, :]
        spoken = speech_mask(tk.reshape(-1), segs).reshape(group_size, span_rows)
        later = tk[:, None, :]
        now = tq[:, :, None]
        allowed = (later <= now) & (later >= now - CTX + 1) & (later >= 0)
        allowed = allowed & (spoken[:, None, :] | (later == now))
        scores = (
            jnp.einsum("bqhd,bkhd->bhqk", queries, keys, preferred_element_type=jnp.float32) * 0.125
        )
        scores = jnp.where(allowed[:, None], scores, -jnp.inf)
        top = jnp.max(scores, axis=-1, keepdims=True)
        expo = jnp.exp(scores - top)
        probs = (expo / jnp.sum(expo, axis=-1, keepdims=True)).astype(jnp.bfloat16)
        out = jnp.einsum("bhqk,bkhd->bqhd", probs, values, preferred_element_type=jnp.float32)
        out = out.reshape(group_size, query_rows, feats).astype(jnp.bfloat16)
        return lax.dynamic_update_slice_in_dim(result, out, first, 0)

    results = lax.fori_loop(0, groups, one_group, empty)
    going_back = jnp.take(results, outgoing, axis=0)
    returned = from_partner(going_back, "tm", top_bit)
    slot_out = jnp.where(mine[:, None, None], results, jnp.take(returned, from_got, axis=0))
    heads_blocks = jnp.einsum(
        "sb,sqf->bqf", select.astype(jnp.bfloat16), slot_out, preferred_element_type=jnp.float32
    )
    heads_out = heads_blocks.astype(jnp.bfloat16).reshape(count_rows, feats)
    attn = jnp.dot(heads_out, w_out, preferred_element_type=jnp.float32)
    xf = x.astype(jnp.float32)
    hidden = jnp.where(speech[:, None], xf + attn, xf)
    conv_in = normalize(hidden, conv_gain).astype(jnp.bfloat16)
    rim = shifted(conv_in[count_rows - (KSZ - 1) :], "tm", 1)
    padded = jnp.concatenate([rim, conv_in], axis=0)
    conv = jnp.zeros((count_rows, width), jnp.float32)
    for shift_by in range(KSZ):
        piece = padded[KSZ - 1 - shift_by : KSZ - 1 - shift_by + count_rows].astype(jnp.float32)
        conv = conv + conv_weight[shift_by][None, :] * piece
    result = jnp.where(speech[:, None], hidden + jax.nn.silu(conv), hidden).astype(jnp.bfloat16)
    return result[None]


def solution(mesh):
    in_specs = (P("rec", "tm", None), P("rec", None, None), P(), P(), P(), P(), P(), P(), P())
    out_specs = P("rec", "tm", None)
    return jax.shard_map(
        per_device, mesh=mesh, in_specs=in_specs, out_specs=out_specs, check_vma=False
    )
```

profile of v0, /device:TPU:16, one launch (start us, length us, event | category | flops | bytes accessed | tf_op | source)
XLA Modules:
  0.0 359.7 jit_solution(12852889600717975443)
XLA Ops:
  0.0 2.3 convert_reduce_fusion
  2.3 2.6 multiply_reduce_fusion.1
  4.9 0.8 multiply_convert_fusion.2
  5.8 1.5 copy-done.5
  7.3 3.8 %collective-permute-start.1 = (bf16[256,1280]{1,0:T(8,128)(2,1)S(1)}, bf16[256,1280]{1,0:T(8,128)(2,1)S(1)}, u32[]{:S(2)}, u32[]{:S(2)}) collective-permute-start(bf16[256,1280]{1,0:T(8,128)(2,1)S(1)} %slice.324), channel_id=1, source_target_pairs={{0,1},{1,2},{2,3},{3,4},{4,5},{5,6},{6,7},{7,8},{8,9},{9,10},{10,1... | collective-permute-start | bytes 1966088 | tf_op jit(solution)/shard_map/ppermute | solution.py:15
  11.8 0.7 convert_reduce_fusion.1
  16.5 2.6 multiply_convert_fusion.1
  19.2 12.7 %collective-permute-done.1 = bf16[256,1280]{1,0:T(8,128)(2,1)S(1)} collective-permute-done((bf16[256,1280]{1,0:T(8,128)(2,1)S(1)}, bf16[256,1280]{1,0:T(8,128)(2,1)S(1)}, u32[]{:S(2)}, u32[]{:S(2)}) %collective-permute-start.1) | collective-permute-done | bytes 655392 | tf_op jit(solution)/shard_map/ppermute | solution.py:15
  32.4 3.6 %pad_maximum_fusion = bf16[8,384,1280]{2,1,0:T(8,128)(2,1)} fusion(bf16[8,128,1280]{2,1,0:T(8,128)(2,1)S(1)} %multiply_convert_fusion.1, bf16[8,128,1280]{2,1,0:T(8,128)(2,1)S(1)} %bitcast.90, bf16[8,128,1280]{2,1,0:T(8,128)(2,1)S(1)} %bitcast.89), kind=kLoop, calls=%fused_computation.65 | loop fusion | flops 23592960 | bytes 15728640 | tf_op jit(solution)/shard_map/concatenate | solution.py:55
  36.0 7.7 %gather_fusion = bf16[8,384,1280]{2,1,0:T(8,128)(2,1)} fusion(bf16[8,384,1280]{2,1,0:T(8,128)(2,1)} %pad_maximum_fusion, s32[1024]{0:T(1024)S(1)} %pad_clamp_fusion.2), kind=kCustom, calls=%fused_computation | custom fusion | bytes 15728672 | tf_op jit(solution)/shard_map/jit(_take)/gather | solution.py:64
  43.7 7.2 %broadcast_select_fusion = bf16[8,384,1280]{2,1,0:T(8,128)(2,1)} fusion(bf16[8,384,1280]{2,1,0:T(8,128)(2,1)} %gather_fusion, pred[8]{0:T(512)(128)(4,1)S(1)} %compare_and_fusion.2), kind=kLoop, calls=%fused_computation.69 | loop fusion | flops 3932160 | bytes 15728648 | tf_op jit(solution)/shard_map/jit(_take)/select_n | solution.py:64
  50.9 6.0 %gather_fusion.1 = bf16[4,384,1280]{2,1,0:T(8,128)(2,1)} fusion(bf16[8,384,1280]{2,1,0:T(8,128)(2,1)} %broadcast_select_fusion, s32[1024]{0:T(1024)S(1)} %pad_clamp_fusion.1), kind=kCustom, calls=%fused_computation.1 | custom fusion | bytes 7864336 | tf_op jit(solution)/shard_map/jit(_take)/gather | solution.py:69
  56.9 4.5 %broadcast_select_fusion.1 = bf16[4,384,1280]{2,1,0:T(8,128)(2,1)} fusion(bf16[4,384,1280]{2,1,0:T(8,128)(2,1)} %gather_fusion.1, pred[4]{0:T(512)(128)(4,1)S(1)} %compare_and_fusion), kind=kLoop, calls=%fused_computation.78 | loop fusion | flops 1966080 | bytes 7864324 | tf_op jit(solution)/shard_map/jit(_take)/select_n | solution.py:69
  61.4 0.6 gather_fusion.3
  62.0 3.6 %collective-permute-start.3 = (s32[4]{0:T(128)S(1)}, s32[4]{0:T(128)S(1)}, u32[]{:S(2)}, u32[]{:S(2)}) collective-permute-start(s32[4]{0:T(128)S(1)} %broadcast_select_fusion.3), channel_id=1, source_target_pairs={{0,64},{1,65},{2,66},{3,67},{4,68},{5,69},{6,70},{7,71},{8,72},{9,... | collective-permute-start | bytes 56 | tf_op jit(solution)/shard_map/ppermute | solution.py:21
  65.6 79.9 %collective-permute-start = (s32[1]{0:T(128)}, s32[1]{0:T(128)}, u32[]{:S(2)}, u32[]{:S(2)}) collective-permute-start(s32[1]{0:T(128)} %bitcast.14), channel_id=1, source_target_pairs={{0,64},{1,65},{2,66},{3,67},{4,68},{5,69},{6,70},{7,71},{8,72},{9,... | collective-permute-start | bytes 20 | tf_op jit(solution)/shard_map/ppermute | solution.py:21
  145.6 3.6 %collective-permute-done = s32[1]{0:T(128)} collective-permute-done((s32[1]{0:T(128)}, s32[1]{0:T(128)}, u32[]{:S(2)}, u32[]{:S(2)}) %collective-permute-start) | collective-permute-done | bytes 36 | tf_op jit(solution)/shard_map/ppermute | solution.py:21
  149.9 0.6 gather_fusion.4
  150.6 6.6 %gather_fusion.2 = bf16[8,384,1280]{2,1,0:T(8,128)(2,1)} fusion(bf16[4,384,1280]{2,1,0:T(8,128)(2,1)} %collective-permute-done.2, s32[1024]{0:T(1024)S(1)} %pad_clamp_fusion), kind=kCustom, calls=%fused_computation.2 | custom fusion | bytes 15728672 | tf_op jit(solution)/shard_map/jit(_take)/gather | solution.py:76
  157.2 8.9 %select_select_fusion = bf16[8,384,1280]{2,1,0:T(8,128)(2,1)} fusion(bf16[8,384,1280]{2,1,0:T(8,128)(2,1)} %gather_fusion.2, pred[8]{0:T(512)(128)(4,1)S(1)} %get-tuple-element.284, pred[8]{0:T(512)(128)(4,1)S(1)} %get-tuple-element.285, bf16[8,384,1280]{2,1,0:T(8,128)(2,1)} %gather_fusion, pred[8]{0:T(512)(128)(4,1)S(1)} %compare_and_fusion.2), kind=kLoop, calls=%fused_computation.68 | loop fusion | flops 11796480 | bytes 23592984 | tf_op jit(solution)/shard_map/jit(_where)/select_n | solution.py:76
  166.1 1.3 broadcast_in_dim.151
  167.4 96.7 %while.15 = (s32[]{:T(128)}, bf16[8,128,640]{1,2,0:T(8,128)(2,1)}, s32[]{:T(128)}, bf16[8,384,1280]{2,1,0:T(8,128)(2,1)}, bf16[1280,640]{1,0:T(8,128)(2,1)}, /*i...) while((s32[]{:T(128)}, bf16[8,128,640]{1,2,0:T(8,128)(2,1)}, ...), condition=%wide.region_11.12_spmd, body=%wide.region_7.11_spmd.sunk | while | flops 6396645376 | bytes 117470656 | solution.py:112
  168.7 1.4 constant_dynamic-slice_fusion.5
  170.1 2.6 convolution_convert_fusion.8
  173.1 2.5 constant_dynamic-slice_fusion.4
  175.8 4.4 %convolution_convert_fusion.9 = bf16[1536,640]{1,0:T(8,128)(2,1)} fusion(bf16[1536,1280]{1,0:T(8,128)(2,1)S(1)} %bitcast.84, bf16[1280,640]{1,0:T(8,128)(2,1)S(1)} %copy-done.29), kind=kOutput, calls=%fused_computation.17.clone.1 | convolution fusion | flops 2517565440 | bytes 7536640 | tf_op jit(solution)/shard_map/while/body/dot_general | solution.py:88
  180.1 4.3 %convolution_convert_fusion.7 = bf16[1536,640]{1,0:T(8,128)(2,1)} fusion(bf16[1536,1280]{1,0:T(8,128)(2,1)S(1)} %bitcast.85, bf16[1280,640]{1,0:T(8,128)(2,1)S(1)} %copy-done.30), kind=kOutput, calls=%fused_computation.16.clone.1 | convolution fusion | flops 2517565440 | bytes 7536640 | tf_op jit(solution)/shard_map/while/body/dot_general | solution.py:87
  184.5 4.0 %copy.47 = bf16[1536,640]{0,1:T(8,128)(2,1)} copy(bf16[1536,640]{1,0:T(8,128)(2,1)} %convolution_convert_fusion.7) | data formatting | bytes 3932160 | tf_op jit(solution)/shard_map/while/body/convert_element_type | solution.py:87
  188.5 4.3 %reshape.451 = bf16[4,384,10,64]{1,0,3,2:T(4,128)(2,1)} reshape(bf16[1536,640]{0,1:T(8,128)(2,1)} %copy.47) | data formatting | bytes 3932160 | tf_op jit(solution)/shard_map/while/body/reshape | solution.py:91
  192.8 4.0 %copy.49 = bf16[1536,640]{0,1:T(8,128)(2,1)} copy(bf16[1536,640]{1,0:T(8,128)(2,1)} %convolution_convert_fusion.9) | data formatting | bytes 3932160 | tf_op jit(solution)/shard_map/while/body/convert_element_type | solution.py:88
  196.9 4.3 %reshape.453 = bf16[4,384,10,64]{1,0,3,2:T(4,128)(2,1)} reshape(bf16[1536,640]{0,1:T(8,128)(2,1)} %copy.49) | data formatting | bytes 3932160 | tf_op jit(solution)/shard_map/while/body/reshape | solution.py:92
  201.2 2.8 fusion.92
  204.0 5.2 %fusion.94 = (f32[4,10,128]{2,1,0:T(8,128)S(1)}, f32[4,10,128,384]{3,2,1,0:T(8,128)}) fusion(f32[4,10,128,384]{3,2,1,0:T(8,128)S(1)} %fusion.92, pred[4,128,384]{2,1,0:T(8,128)(4,1)S(1)} %or_and_fusion.2), kind=kOutput, calls=%fused_computation.191.clone.1 | output fusion | flops 11796863 | bytes 15945728 | tf_op jit(solution)/shard_map/while/body/sub | solution.py:106
  209.2 5.3 %fusion.95 = bf16[4,10,64,128]{3,2,1,0:T(8,128)(2,1)S(1)} fusion(f32[4,10,128,384]{3,2,1,0:T(8,128)} %get-tuple-element.356, f32[4,10,128]{2,1,0:T(8,128)S(1)} %get-tuple-element.357, bf16[4,384,10,64]{1,0,3,2:T(4,128)(2,1)S(1)} %copy-done.1), kind=kOutput, calls=%fused_computation.22.clone.1 | convolution fusion | flops 255918080 | bytes 10506240 | tf_op jit(solution)/shard_map/while/body/bhqk,bkhd->bqhd/dot_general | solution.py:108
  214.6 1.1 copy-done.9
  217.0 1.4 constant_dynamic-slice_fusion.5
  218.4 2.6 convolution_convert_fusion.8
  221.5 2.5 constant_dynamic-slice_fusion.4
  224.1 4.4 %convolution_convert_fusion.9 = bf16[1536,640]{1,0:T(8,128)(2,1)} fusion(bf16[1536,1280]{1,0:T(8,128)(2,1)S(1)} %bitcast.84, bf16[1280,640]{1,0:T(8,128)(2,1)S(1)} %copy-done.29), kind=kOutput, calls=%fused_computation.17.clone.1 | convolution fusion | flops 2517565440 | bytes 7536640 | tf_op jit(solution)/shard_map/while/body/dot_general | solution.py:88
  228.5 4.3 %convolution_convert_fusion.7 = bf16[1536,640]{1,0:T(8,128)(2,1)} fusion(bf16[1536,1280]{1,0:T(8,128)(2,1)S(1)} %bitcast.85, bf16[1280,640]{1,0:T(8,128)(2,1)S(1)} %copy-done.30), kind=kOutput, calls=%fused_computation.16.clone.1 | convolution fusion | flops 2517565440 | bytes 7536640 | tf_op jit(solution)/shard_map/while/body/dot_general | solution.py:87
  232.8 4.0 %copy.47 = bf16[1536,640]{0,1:T(8,128)(2,1)} copy(bf16[1536,640]{1,0:T(8,128)(2,1)} %convolution_convert_fusion.7) | data formatting | bytes 3932160 | tf_op jit(solution)/shard_map/while/body/convert_element_type | solution.py:87
  236.9 4.3 %reshape.451 = bf16[4,384,10,64]{1,0,3,2:T(4,128)(2,1)} reshape(bf16[1536,640]{0,1:T(8,128)(2,1)} %copy.47) | data formatting | bytes 3932160 | tf_op jit(solution)/shard_map/while/body/reshape | solution.py:91
  241.2 4.0 %copy.49 = bf16[1536,640]{0,1:T(8,128)(2,1)} copy(bf16[1536,640]{1,0:T(8,128)(2,1)} %convolution_convert_fusion.9) | data formatting | bytes 3932160 | tf_op jit(solution)/shard_map/while/body/convert_element_type | solution.py:88
  245.2 4.3 %reshape.453 = bf16[4,384,10,64]{1,0,3,2:T(4,128)(2,1)} reshape(bf16[1536,640]{0,1:T(8,128)(2,1)} %copy.49) | data formatting | bytes 3932160 | tf_op jit(solution)/shard_map/while/body/reshape | solution.py:92
  249.6 2.8 fusion.92
  252.3 5.2 %fusion.94 = (f32[4,10,128]{2,1,0:T(8,128)S(1)}, f32[4,10,128,384]{3,2,1,0:T(8,128)}) fusion(f32[4,10,128,384]{3,2,1,0:T(8,128)S(1)} %fusion.92, pred[4,128,384]{2,1,0:T(8,128)(4,1)S(1)} %or_and_fusion.2), kind=kOutput, calls=%fused_computation.191.clone.1 | output fusion | flops 11796863 | bytes 15945728 | tf_op jit(solution)/shard_map/while/body/sub | solution.py:106
  257.6 5.3 %fusion.95 = bf16[4,10,64,128]{3,2,1,0:T(8,128)(2,1)S(1)} fusion(f32[4,10,128,384]{3,2,1,0:T(8,128)} %get-tuple-element.356, f32[4,10,128]{2,1,0:T(8,128)S(1)} %get-tuple-element.357, bf16[4,384,10,64]{1,0,3,2:T(4,128)(2,1)S(1)} %copy-done.1), kind=kOutput, calls=%fused_computation.22.clone.1 | convolution fusion | flops 255918080 | bytes 10506240 | tf_op jit(solution)/shard_map/while/body/bhqk,bkhd->bqhd/dot_general | solution.py:108
  263.0 1.1 copy-done.9
  264.1 3.0 gather_fusion.5
  267.1 1.2 broadcast_select_fusion.2
  268.3 0.6 collective-permute-start.4
  269.2 11.6 %collective-permute-done.4 = bf16[4,128,640]{1,2,0:T(8,128)(2,1)} collective-permute-done((bf16[4,128,640]{1,2,0:T(8,128)(2,1)S(1)}, bf16[4,128,640]{1,2,0:T(8,128)(2,1)}, u32[]{:S(2)}, u32[]{:S(2)}) %collective-permute-start.4) | collective-permute-done | bytes 655392 | tf_op jit(solution)/shard_map/ppermute | solution.py:21
  280.8 3.0 gather_fusion.6
  283.8 2.6 select_select_fusion.1
  286.4 2.2 copy.28
  289.4 1.0 copy-done.4
  290.4 2.6 fusion.60
  293.1 0.7 multiply_reduce_fusion
  293.8 0.7 multiply_convert_fusion
  294.5 0.9 copy-done.2
  295.4 1.5 copy-done.7
  296.9 1.9 collective-permute-start.5
  298.9 8.5 %collective-permute-done.5 = bf16[30,1280]{1,0:T(8,128)(2,1)S(1)} collective-permute-done((bf16[30,1280]{1,0:T(8,128)(2,1)S(1)}, bf16[30,1280]{1,0:T(8,128)(2,1)S(1)}, u32[]{:S(2)}, u32[]{:S(2)}) %collective-permute-start.5) | collective-permute-done | bytes 76832 | tf_op jit(solution)/shard_map/ppermute | solution.py:15
  307.4 52.2 %fusion.46 = bf16[1,1024,1280]{2,1,0:T(8,128)(2,1)} fusion(f32[1024,1280]{1,0:T(8,128)} %copy-done.2, bf16[1024,1280]{1,0:T(8,128)(2,1)} %copy-done.7, bf16[30,1280]{1,0:T(8,128)(2,1)S(1)} %collective-permute-done.5, f32[1280]{0:T(1024)S(1)} %get-tuple-element.244, f32[1280]{0:T(1024)S(1)} %get-tuple-element.245, f32[1280]{0:T(1024)S(1)} %get-tuple-element.216, ...), kind=kLoop, calls=%fused_computation.117 | loop fusion | flops 247726080 | bytes 10722304 | tf_op jit(solution)/shard_map/broadcast_in_dim | solution.py:131
  (124 shorter events, 7.1 us)
Async XLA Ops:
  0.0 289.4 %copy-start = (bf16[640,1280]{1,0:T(8,128)(2,1)S(1)}, bf16[640,1280]{1,0:T(8,128)(2,1)}, u32[]{:S(2)}) copy-start(bf16[640,1280]{1,0:T(8,128)(2,1)} %param.17) | copy-start | bytes 4915204
  0.0 4.9 %copy-start.3 = (bf16[1,1024,1280]{2,1,0:T(8,128)(2,1)S(1)}, bf16[1,1024,1280]{2,1,0:T(8,128)(2,1)}, u32[]{:S(2)}) copy-start(bf16[1,1024,1280]{2,1,0:T(8,128)(2,1)} %param.11) | copy-start | bytes 7864324
  0.0 4.9 %copy-start.13 = (f32[1280]{0:T(1024)S(1)}, f32[1280]{0:T(1024)}, u32[]{:S(2)}) copy-start(f32[1280]{0:T(1024)} %param.13) | copy-start | bytes 15364
  2.3 8.9 %copy-start.12 = (s32[1,256,2]{1,2,0:T(2,128)S(1)}, s32[1,256,2]{1,2,0:T(2,128)}, u32[]{:S(2)}) copy-start(s32[1,256,2]{1,2,0:T(2,128)} %param.12) | copy-start | bytes 6148
  5.8 1.5 copy-start.5
  7.3 24.6 %collective-permute-start.1 = (bf16[256,1280]{1,0:T(8,128)(2,1)S(1)}, bf16[256,1280]{1,0:T(8,128)(2,1)S(1)}, u32[]{:S(2)}, u32[]{:S(2)}) collective-permute-start(bf16[256,1280]{1,0:T(8,128)(2,1)S(1)} %slice.324), channel_id=1, source_target_pairs={{0,1},{1,2},{2,3},{3,4},{4,5},{5,6},{6,7},{7,8},{8,9},{9,10},{10,1... | collective-permute-start | bytes 1966088 | tf_op jit(solution)/shard_map/ppermute | solution.py:15
  11.6 4.9 %copy-start.17 = (pred[1024]{0:T(1024)(128)(4,1)}, pred[1024]{0:T(1024)(128)(4,1)S(1)}, u32[]{:S(2)}) copy-start(pred[1024]{0:T(1024)(128)(4,1)S(1)} %and_reduce_fusion.1) | copy-start | bytes 3076
  15.6 41.3 %copy-start.19 = (pred[4]{0:T(512)(128)(4,1)}, pred[4]{0:T(512)(128)(4,1)S(1)}, u32[]{:S(2)}) copy-start(pred[4]{0:T(512)(128)(4,1)S(1)} %compare_and_fusion) | copy-start | bytes 16
  15.6 0.9 copy-start.25
  15.8 16.1 %copy-start.6 = (bf16[1024,1280]{1,0:T(8,128)(2,1)S(1)}, bf16[1024,1280]{1,0:T(8,128)(2,1)}, u32[]{:S(2)}) copy-start(bf16[1024,1280]{1,0:T(8,128)(2,1)} %copy-done.5) | copy-start | bytes 7864324
  15.8 0.6 copy-start.27
  16.5 44.8 %copy-start.16 = (s32[1024]{0:T(1024)}, s32[1024]{0:T(1024)S(1)}, u32[]{:S(2)}) copy-start(s32[1024]{0:T(1024)S(1)} %pad_clamp_fusion.1) | copy-start | bytes 12292
  61.3 89.2 %collective-permute-start.2 = (bf16[4,384,1280]{2,1,0:T(8,128)(2,1)}, bf16[4,384,1280]{2,1,0:T(8,128)(2,1)}, u32[]{:S(2)}, u32[]{:S(2)}) collective-permute-start(bf16[4,384,1280]{2,1,0:T(8,128)(2,1)} %broadcast_select_fusion.1), channel_id=1, source_target_pairs={{0,64},{1,65},{2,66},{3,67},{4,68},{5,69},{6,70},{7,71},{8,72},{9,... | collective-permute-start | bytes 11796488 | tf_op jit(solution)/shard_map/ppermute | solution.py:21
  62.0 87.9 %collective-permute-start.3 = (s32[4]{0:T(128)S(1)}, s32[4]{0:T(128)S(1)}, u32[]{:S(2)}, u32[]{:S(2)}) collective-permute-start(s32[4]{0:T(128)S(1)} %broadcast_select_fusion.3), channel_id=1, source_target_pairs={{0,64},{1,65},{2,66},{3,67},{4,68},{5,69},{6,70},{7,71},{8,72},{9,... | collective-permute-start | bytes 56 | tf_op jit(solution)/shard_map/ppermute | solution.py:21
  65.6 83.6 %collective-permute-start = (s32[1]{0:T(128)}, s32[1]{0:T(128)}, u32[]{:S(2)}, u32[]{:S(2)}) collective-permute-start(s32[1]{0:T(128)} %bitcast.14), channel_id=1, source_target_pairs={{0,64},{1,65},{2,66},{3,67},{4,68},{5,69},{6,70},{7,71},{8,72},{9,... | collective-permute-start | bytes 20 | tf_op jit(solution)/shard_map/ppermute | solution.py:21
  145.6 11.6 %copy-start.21 = (pred[8]{0:T(512)(128)(4,1)}, pred[8]{0:T(512)(128)(4,1)S(1)}, u32[]{:S(2)}) copy-start(pred[8]{0:T(512)(128)(4,1)S(1)} %get-tuple-element.284) | copy-start | bytes 28
  145.6 11.6 %copy-start.23 = (pred[8]{0:T(512)(128)(4,1)}, pred[8]{0:T(512)(128)(4,1)S(1)}, u32[]{:S(2)}) copy-start(pred[8]{0:T(512)(128)(4,1)S(1)} %get-tuple-element.285) | copy-start | bytes 28
  145.6 11.6 %copy-start.15 = (s32[1024]{0:T(1024)}, s32[1024]{0:T(1024)S(1)}, u32[]{:S(2)}) copy-start(s32[1024]{0:T(1024)S(1)} %pad_clamp_fusion) | copy-start | bytes 12292
  167.4 99.7 %copy-start.20 = (pred[4]{0:T(512)(128)(4,1)S(1)}, pred[4]{0:T(512)(128)(4,1)}, u32[]{:S(2)}) copy-start(pred[4]{0:T(512)(128)(4,1)} %copy-done.19) | copy-start | bytes 16
  167.4 101.6 %copy-start.11 = (f32[31,1280]{1,0:T(8,128)S(1)}, f32[31,1280]{1,0:T(8,128)}, u32[]{:S(2)}) copy-start(f32[31,1280]{1,0:T(8,128)} %param.19) | copy-start | bytes 476164
  173.1 2.6 copy-start.29
  175.7 4.4 %copy-start.30 = (bf16[1280,640]{1,0:T(8,128)(2,1)S(1)}, bf16[1280,640]{1,0:T(8,128)(2,1)}, u32[]{:S(2)}) copy-start(bf16[1280,640]{1,0:T(8,128)(2,1)} %get-tuple-element.394) | copy-start | bytes 4915204 | tf_op jit(solution)/shard_map/while
  204.0 5.2 %copy-start.1 = (bf16[4,384,10,64]{1,0,3,2:T(4,128)(2,1)S(1)}, bf16[4,384,10,64]{1,0,3,2:T(4,128)(2,1)}, u32[]{:S(2)}) copy-start(bf16[4,384,10,64]{1,0,3,2:T(4,128)(2,1)} %reshape.453) | copy-start | bytes 5898244 | tf_op jit(solution)/shard_map/while
  209.2 5.3 %copy-start.8 = (bf16[8,128,640]{1,2,0:T(8,128)(2,1)S(1)}, bf16[8,128,640]{1,2,0:T(8,128)(2,1)}, u32[]{:S(2)}) copy-start(bf16[8,128,640]{1,2,0:T(8,128)(2,1)} %get-tuple-element.373) | copy-start | bytes 3932164 | tf_op jit(solution)/shard_map/while
  214.6 1.1 copy-start.9
  221.5 2.6 copy-start.29
  224.1 4.4 %copy-start.30 = (bf16[1280,640]{1,0:T(8,128)(2,1)S(1)}, bf16[1280,640]{1,0:T(8,128)(2,1)}, u32[]{:S(2)}) copy-start(bf16[1280,640]{1,0:T(8,128)(2,1)} %get-tuple-element.394) | copy-start | bytes 4915204 | tf_op jit(solution)/shard_map/while
  252.3 5.2 %copy-start.1 = (bf16[4,384,10,64]{1,0,3,2:T(4,128)(2,1)S(1)}, bf16[4,384,10,64]{1,0,3,2:T(4,128)(2,1)}, u32[]{:S(2)}) copy-start(bf16[4,384,10,64]{1,0,3,2:T(4,128)(2,1)} %reshape.453) | copy-start | bytes 5898244 | tf_op jit(solution)/shard_map/while
  257.6 5.3 %copy-start.8 = (bf16[8,128,640]{1,2,0:T(8,128)(2,1)S(1)}, bf16[8,128,640]{1,2,0:T(8,128)(2,1)}, u32[]{:S(2)}) copy-start(bf16[8,128,640]{1,2,0:T(8,128)(2,1)} %get-tuple-element.373) | copy-start | bytes 3932164 | tf_op jit(solution)/shard_map/while
  263.0 1.1 copy-start.9
  264.1 19.7 %copy-start.10 = (bf16[8,128,640]{1,2,0:T(8,128)(2,1)S(1)}, bf16[8,128,640]{1,2,0:T(8,128)(2,1)}, u32[]{:S(2)}) copy-start(bf16[8,128,640]{1,2,0:T(8,128)(2,1)} %get-tuple-element.214) | copy-start | bytes 3932164
  264.1 19.7 %copy-start.22 = (pred[8]{0:T(512)(128)(4,1)S(1)}, pred[8]{0:T(512)(128)(4,1)}, u32[]{:S(2)}) copy-start(pred[8]{0:T(512)(128)(4,1)} %copy-done.21) | copy-start | bytes 28
  264.1 19.7 %copy-start.24 = (pred[8]{0:T(512)(128)(4,1)S(1)}, pred[8]{0:T(512)(128)(4,1)}, u32[]{:S(2)}) copy-start(pred[8]{0:T(512)(128)(4,1)} %copy-done.23) | copy-start | bytes 28
  267.1 21.5 %copy-start.26 = (pred[8]{0:T(512)(128)(4,1)S(1)}, pred[8]{0:T(512)(128)(4,1)}, u32[]{:S(2)}) copy-start(pred[8]{0:T(512)(128)(4,1)} %copy-done.25) | copy-start | bytes 28
  267.1 21.5 %copy-start.28 = (s32[8]{0:T(128)S(1)}, s32[8]{0:T(128)}, u32[]{:S(2)}) copy-start(s32[8]{0:T(128)} %copy-done.27) | copy-start | bytes 100
  268.3 12.5 %collective-permute-start.4 = (bf16[4,128,640]{1,2,0:T(8,128)(2,1)S(1)}, bf16[4,128,640]{1,2,0:T(8,128)(2,1)}, u32[]{:S(2)}, u32[]{:S(2)}) collective-permute-start(bf16[4,128,640]{1,2,0:T(8,128)(2,1)S(1)} %broadcast_select_fusion.2), channel_id=1, source_target_pairs={{0,64},{1,65},{2,66},{3,67},{4,68},{5,69},{6,70},{7,71},{8,72},{9,... | collective-permute-start | bytes 1966088 | tf_op jit(solution)/shard_map/ppermute | solution.py:21
  283.8 5.6 %copy-start.18 = (pred[1024]{0:T(1024)(128)(4,1)S(1)}, pred[1024]{0:T(1024)(128)(4,1)}, u32[]{:S(2)}) copy-start(pred[1024]{0:T(1024)(128)(4,1)} %copy-done.17) | copy-start | bytes 3076
  288.6 1.7 copy-start.4
  293.0 2.3 copy-start.2
  293.0 0.7 copy-start.14
  295.3 1.5 copy-start.7
  296.9 10.5 %collective-permute-start.5 = (bf16[30,1280]{1,0:T(8,128)(2,1)S(1)}, bf16[30,1280]{1,0:T(8,128)(2,1)S(1)}, u32[]{:S(2)}, u32[]{:S(2)}) collective-permute-start(bf16[30,1280]{1,0:T(8,128)(2,1)S(1)} %slice.327), channel_id=1, source_target_pairs={{0,1},{1,2},{2,3},{3,4},{4,5},{5,6},{6,7},{7,8},{8,9},{9,10},{10,1... | collective-permute-start | bytes 230408 | tf_op jit(solution)/shard_map/ppermute | solution.py:15
where the time goes:
time: 364 us; the launch traced here: 360 us
  other arithmetic  105 us (29%)
  starting transfers between devices  89.9 us (25%)
  local copies, waits for them, and re-layouts  82 us (23%)
  matrix products  42 us (12%)
  waiting for transfers between devices  36.4 us (10%)
  between operations  4.37 us (1%)
    ppermute x4, starting transfers between devices, from_partner(): return lax.ppermute(value, axis, pairs)  84.2 us
    broadcast_in_dim x1, other arithmetic, per_device(): return result[None]  52.2 us
    ppermute x2, waiting for transfers between devices, shifted(): return lax.ppermute(shard, axis, pairs)  21.2 us
    ppermute x4, waiting for transfers between devices, from_partner(): return lax.ppermute(value, axis, pairs)  15.2 us
    dot_general x2, matrix products, one_group(): jnp.einsum('bhqk,bkhd->bqhd', probs, values, preferred_element_type=jnp.f...  10.5 us
    sub x2, other arithmetic, one_group(): expo = jnp.exp(scores - top)  10.5 us
    select_n x1, other arithmetic, per_device(): jnp.where(mine[:, None, None], own_windows, jnp.take(got_rows, from_got,...  8.87 us
    dot_general x2, matrix products, one_group(): jnp.dot(flat, w_value, preferred_element_type=jnp.float32)  8.76 us
  transfers between devices with their start and end apart: 6, of which 4 were waited for; matrix products, arithmetic and copies ran while one was open for 2% of the time, Pallas kernels for 0%

commit v1 on v0

v1 whole, which is shorter than its diff:
```python
import jax
import jax.experimental.pallas as pl
import jax.experimental.pallas.tpu as pltpu
import jax.numpy as jnp
from jax import lax
from jax.sharding import PartitionSpec as P

H = 10
HS = 64
CTX = 256
KSZ = 31
ROWS = 256
HALO = 32
EXTRA = CTX + HALO
LANES = 128
SCALE = 0.125 * 1.4426950408889634
NEG = -1e30


def norm(values, gain):
    mean = jnp.mean(values, axis=-1, keepdims=True)
    centred = values - mean
    var = jnp.mean(centred * centred, axis=-1, keepdims=True)
    return centred * lax.rsqrt(var + 1e-05) * gain


def norm_rows(src, dst, first, count, gain_ref, step=16):
    def body(i, carry):
        rows = pl.ds(pl.multiple_of(first + i * step, 16), step)
        v = src[rows, :].astype(jnp.float32)
        dst[rows, :] = norm(v, gain_ref[...]).astype(jnp.bfloat16)
        return carry

    lax.fori_loop(0, count // step, body, 0)


def tri_masks(rows):
    i = lax.broadcasted_iota(jnp.int32, (rows, ROWS), 0)
    j = lax.broadcasted_iota(jnp.int32, (rows, ROWS), 1)
    return j <= i


def bias_row(flags, marks):
    lane = lax.broadcasted_iota(jnp.int32, (1, ROWS), 1)
    row = jnp.full((1, ROWS), NEG, jnp.float32)
    for upto, flag in reversed(marks):
        row = jnp.where(lane < upto, jnp.where(flags[flag] > 0, 0.0, NEG), row)
    return row


def attend(q_ref, q_first, k_ref, v_ref, prev_first, rows, bias, tri, heads_ref, out_first):
    cur_first = prev_first + ROWS
    lane = lax.broadcasted_iota(jnp.int32, (rows, LANES), 1)
    tri01 = jnp.where(tri, 1.0, 0.0).astype(jnp.bfloat16)
    ones = jnp.ones((ROWS, LANES), jnp.bfloat16)
    zero = jnp.zeros((rows, LANES), jnp.bfloat16)
    for pair in range(H // 2):
        cols = slice(pair * LANES, (pair + 1) * LANES)
        q = q_ref[pl.ds(q_first, rows), cols]
        kp = k_ref[pl.ds(prev_first, ROWS), cols]
        kc = k_ref[pl.ds(cur_first, ROWS), cols]
        vp = jnp.concatenate([v_ref[pl.ds(prev_first, ROWS), cols], ones], axis=1)
        vc = jnp.concatenate([v_ref[pl.ds(cur_first, ROWS), cols], ones], axis=1)
        outs = []
        for half in range(2):
            mine = (lane < HS) if half == 0 else (lane >= HS)
            qh = jnp.where(mine, q, zero)
            dims = (((1,), (1,)), ((), ()))
            sp = lax.dot_general(qh, kp, dims, preferred_element_type=jnp.float32)
            sc = lax.dot_general(qh, kc, dims, preferred_element_type=jnp.float32)
            s = jnp.where(tri, sc, sp) + bias
            top = jnp.max(s, axis=-1, keepdims=True)
            p = jnp.exp2((s - top) * SCALE).astype(jnp.bfloat16)
            pc = p * tri01
            pp = p - pc
            outs.append(
                jnp.dot(pp, vp, preferred_element_type=jnp.float32)
                + jnp.dot(pc, vc, preferred_element_type=jnp.float32)
            )
        first = lane < HS
        num = jnp.where(first, outs[0][:, :LANES], outs[1][:, :LANES])
        den = jnp.where(first, outs[0][:, LANES:], outs[1][:, LANES:])
        heads_ref[pl.ds(out_first, rows), cols] = (num / den).astype(jnp.bfloat16)


def conv_tile(cbuf, w, c, base, rows):
    acc = [None] * (rows // 8)
    for res in range(8):
        for n in range(-3, rows // 8):
            x = cbuf[c, pl.ds(base + HALO + 8 * n - res, 8), :]
            for m in range(4):
                tap = 8 * m + res
                if tap < KSZ and 0 <= n + m < rows // 8:
                    t = w[tap] * x
                    acc[n + m] = t if acc[n + m] is None else acc[n + m] + t
    return acc


def residual(x_ref, x_first, attn_ref, flags, marks, hid_ref, hid_first, cbuf, cbuf_first, gain_ref, scale=None):
    step = 16
    at = 0
    for upto, flag in marks:
        on = flags[flag] > 0

        def body(i, carry, at=at, on=on):
            here = at + i * step
            xf = x_ref[pl.ds(pl.multiple_of(x_first + here, 16), step), :].astype(jnp.float32)
            attn = attn_ref[pl.ds(pl.multiple_of(here, 16), step), :]
            hidden = jnp.where(on, xf + attn, xf)
            if hid_ref is not None:
                hid_ref[pl.ds(pl.multiple_of(hid_first + here, 16), step), :] = hidden
            cin = norm(hidden, gain_ref[...]).astype(jnp.bfloat16).astype(jnp.float32)
            if scale is not None:
                cin = cin * scale
            for c in range(10):
                cbuf[c, pl.ds(pl.multiple_of(cbuf_first + here, 16), step), :] = cin[:, c * LANES : (c + 1) * LANES]
            return carry

        lax.fori_loop(0, (upto - at) // step, body, 0)
        at = upto


def conv_rows(cbuf, w_ref, hid_ref, hid_off, flags, first, count, rows, out_ref, out_off):
    def lanes(c, carry):
        cols = pl.ds(pl.multiple_of(c * LANES, LANES), LANES)
        w = [jnp.broadcast_to(w_ref[pl.ds(j, 1), cols], (8, LANES)) for j in range(KSZ)]

        def chunk(r, inner):
            base = pl.multiple_of(first + r * rows, 32)
            acc = jnp.concatenate(conv_tile(cbuf, w, c, base, rows), axis=0)
            on = flags[3 + base // LANES] > 0
            hidden = hid_ref[pl.ds(pl.multiple_of(base + hid_off, 32), rows), cols]
            silu = acc / (1.0 + jnp.exp(-acc))
            out = jnp.where(on, hidden + silu, hidden)
            out_ref[pl.ds(pl.multiple_of(base + out_off, 32), rows), cols] = out.astype(jnp.bfloat16)
            return inner

        lax.fori_loop(0, count // rows, chunk, 0)
        return carry

    lax.fori_loop(0, 10, lanes, 0)


def kernel_a(flags, x_hbm, wq_hbm, wk_hbm, wv_hbm, wo_hbm, g1, g2, cw, out_hbm, q0, k0, v0, hid0, cin0,
             x, wqkv, wo, normed, q, k, v, heads, attn, hid, cbuf, out, sems):
    feats = H * HS
    copies = [
        pltpu.make_async_copy(x_hbm, x, sems.at[0]),
        pltpu.make_async_copy(wq_hbm, wqkv.at[:, pl.ds(0, feats)], sems.at[1]),
        pltpu.make_async_copy(wk_hbm, wqkv.at[:, pl.ds(feats, feats)], sems.at[2]),
        pltpu.make_async_copy(wv_hbm, wqkv.at[:, pl.ds(2 * feats, feats)], sems.at[3]),
        pltpu.make_async_copy(wo_hbm, wo, sems.at[4]),
    ]
    for copy in copies:
        copy.start()
    copies[0].wait()
    norm_rows(x, normed, 0, 1024, g1)
    for copy in copies[1:]:
        copy.wait()
    for b in range(4):
        rows = pl.ds(b * ROWS, ROWS)
        for part, dst in enumerate((q, k, v)):
            dst[rows, :] = jnp.dot(
                normed[rows, :], wqkv[:, part * feats : (part + 1) * feats], preferred_element_type=jnp.float32
            ).astype(jnp.bfloat16)
    q0[...] = q[0:ROWS, :]
    k0[...] = k[0:ROWS, :]
    v0[...] = v[0:ROWS, :]
    tri = tri_masks(ROWS)
    for b in range(1, 4):
        f = 3 + 2 * b
        bias = jnp.where(
            tri,
            bias_row(flags, [(128, f), (256, f + 1)]),
            bias_row(flags, [(128, f - 2), (256, f - 1)]),
        )
        attend(q, b * ROWS, k, v, (b - 1) * ROWS, ROWS, bias, tri, heads, 0)
        attn[...] = jnp.dot(heads[...], wo[...], preferred_element_type=jnp.float32)
        residual(x, b * ROWS, attn, flags, [(128, f), (256, f + 1)], hid, b * ROWS, cbuf, HALO + b * ROWS, g2)
    hid0[...] = hid[pl.ds(ROWS, HALO), :]
    cin0[...] = cbuf[:, pl.ds(HALO + ROWS, HALO), :]
    conv_rows(cbuf, cw, hid, 0, flags, EXTRA, 1024 - EXTRA, 32, out, 0)
    done = pltpu.make_async_copy(out.at[pl.ds(EXTRA, 1024 - EXTRA), :], out_hbm.at[pl.ds(EXTRA, 1024 - EXTRA), :], sems.at[5])
    done.start()
    done.wait()


def kernel_b(flags, x_hbm, tail, wq_hbm, wk_hbm, wv_hbm, wo_hbm, g1, g2, cw, q0, k0, v0, hid0, cin0, _, out_hbm,
             x, wqkv, wo, normed, q, k, v, heads, attn, hid, cbuf, out, sems):
    feats = H * HS
    copies = [
        pltpu.make_async_copy(x_hbm.at[pl.ds(0, ROWS), :], x, sems.at[0]),
        pltpu.make_async_copy(wq_hbm, wqkv.at[:, pl.ds(0, feats)], sems.at[1]),
        pltpu.make_async_copy(wk_hbm, wqkv.at[:, pl.ds(feats, feats)], sems.at[2]),
        pltpu.make_async_copy(wv_hbm, wqkv.at[:, pl.ds(2 * feats, feats)], sems.at[3]),
        pltpu.make_async_copy(wo_hbm, wo, sems.at[4]),
    ]
    for copy in copies:
        copy.start()
    norm_rows(tail, normed, 0, EXTRA, g1)
    k[pl.ds(EXTRA, ROWS), :] = k0[...]
    v[pl.ds(EXTRA, ROWS), :] = v0[...]
    q[pl.ds(HALO, ROWS), :] = q0[...]
    for copy in copies:
        copy.wait()
    q[pl.ds(0, HALO), :] = jnp.dot(
        normed[pl.ds(CTX, HALO), :], wqkv[:, :feats], preferred_element_type=jnp.float32
    ).astype(jnp.bfloat16)
    for part, dst in ((1, k), (2, v)):
        dst[pl.ds(0, EXTRA), :] = jnp.dot(
            normed[...], wqkv[:, part * feats : (part + 1) * feats], preferred_element_type=jnp.float32
        ).astype(jnp.bfloat16)
    small = tri_masks(HALO)
    bias = jnp.where(
        small, bias_row(flags, [(HALO, 2)]), bias_row(flags, [(HALO, 0), (HALO + 128, 1), (256, 2)])
    )
    attend(q, 0, k, v, 0, HALO, bias, small, heads, 0)
    tri = tri_masks(ROWS)
    bias = jnp.where(
        tri, bias_row(flags, [(128, 3), (256, 4)]), bias_row(flags, [(128, 1), (256, 2)])
    )
    attend(q, HALO, k, v, HALO, ROWS, bias, tri, heads, HALO)
    attn[...] = jnp.dot(heads[...], wo[...], preferred_element_type=jnp.float32)
    keep = jnp.where(flags[11] > 0, 1.0, 0.0)
    residual(tail, CTX, attn, flags, [(HALO, 2)], None, 0, cbuf, 0, g2, keep)
    residual(x, 0, attn.at[pl.ds(HALO, ROWS), :], flags, [(128, 3), (256, 4)], hid, 0, cbuf, HALO, g2)
    hid[pl.ds(ROWS, HALO), :] = hid0[...]
    cbuf[:, pl.ds(HALO + ROWS, HALO), :] = cin0[...]
    conv_rows(cbuf, cw, hid, 0, flags, 0, EXTRA, 32, out, 0)
    done = pltpu.make_async_copy(out, out_hbm.at[pl.ds(0, EXTRA), :], sems.at[5])
    done.start()
    done.wait()


def per_device(frames, segments, ln_gain, w_query, w_key, w_value, w_out, conv_gain, conv_weight):
    x = frames[0]
    segs = segments[0]
    count, width = x.shape
    feats = H * HS
    peers = lax.axis_size("tm")
    me = lax.axis_index("tm")
    tail = lax.ppermute(x[count - EXTRA :], "tm", [(i, i + 1) for i in range(peers - 1)])
    starts = me * count + (jnp.arange(11, dtype=jnp.int32) - 3) * LANES
    inside = (starts[:, None] >= segs[None, :, 0]) & (starts[:, None] < segs[None, :, 1])
    flags = jnp.concatenate([jnp.any(inside, axis=1).astype(jnp.int32), jnp.minimum(me, 1).reshape(1).astype(jnp.int32)])
    g1 = ln_gain.reshape(1, width)
    g2 = conv_gain.reshape(1, width)
    hbm = pl.BlockSpec(memory_space=pl.ANY)
    vmem = pl.BlockSpec(memory_space=pltpu.VMEM)
    smem = pl.BlockSpec(memory_space=pltpu.SMEM)
    bf16, f32 = jnp.bfloat16, jnp.float32
    out, q0, k0, v0, hid0, cin0 = pl.pallas_call(
        kernel_a,
        in_specs=[smem, hbm, hbm, hbm, hbm, hbm, vmem, vmem, vmem],
        out_specs=[hbm] + [vmem] * 5,
        out_shape=[
            jax.ShapeDtypeStruct((count, width), bf16),
            jax.ShapeDtypeStruct((ROWS, feats), bf16),
            jax.ShapeDtypeStruct((ROWS, feats), bf16),
            jax.ShapeDtypeStruct((ROWS, feats), bf16),
            jax.ShapeDtypeStruct((HALO, width), f32),
            jax.ShapeDtypeStruct((10, HALO, LANES), f32),
        ],
        scratch_shapes=[
            pltpu.VMEM((count, width), bf16),
            pltpu.VMEM((width, 3 * feats), bf16),
            pltpu.VMEM((feats, width), bf16),
            pltpu.VMEM((count, width), bf16),
            pltpu.VMEM((count, feats), bf16),
            pltpu.VMEM((count, feats), bf16),
            pltpu.VMEM((count, feats), bf16),
            pltpu.VMEM((ROWS, feats), bf16),
            pltpu.VMEM((ROWS, width), f32),
            pltpu.VMEM((count, width), f32),
            pltpu.VMEM((10, HALO + count, LANES), f32),
            pltpu.VMEM((count, width), bf16),
            pltpu.SemaphoreType.DMA((6,)),
        ],
        compiler_params=pltpu.CompilerParams(vmem_limit_bytes=56 << 20),
        cost_estimate=pl.CostEstimate(flops=12_000_000_000, bytes_accessed=11_000_000, transcendentals=4_000_000),
        name="own_rows",
    )(flags, x, w_query, w_key, w_value, w_out, g1, g2, conv_weight)
    out = pl.pallas_call(
        kernel_b,
        in_specs=[smem, hbm, vmem, hbm, hbm, hbm, hbm] + [vmem] * 8 + [hbm],
        out_specs=hbm,
        out_shape=jax.ShapeDtypeStruct((count, width), bf16),
        input_output_aliases={15: 0},
        scratch_shapes=[
            pltpu.VMEM((ROWS, width), bf16),
            pltpu.VMEM((width, 3 * feats), bf16),
            pltpu.VMEM((feats, width), bf16),
            pltpu.VMEM((EXTRA, width), bf16),
            pltpu.VMEM((EXTRA, feats), bf16),
            pltpu.VMEM((EXTRA + ROWS, feats), bf16),
            pltpu.VMEM((EXTRA + ROWS, feats), bf16),
            pltpu.VMEM((EXTRA, feats), bf16),
            pltpu.VMEM((EXTRA, width), f32),
            pltpu.VMEM((EXTRA, width), f32),
            pltpu.VMEM((10, HALO + EXTRA, LANES), f32),
            pltpu.VMEM((EXTRA, width), bf16),
            pltpu.SemaphoreType.DMA((6,)),
        ],
        compiler_params=pltpu.CompilerParams(vmem_limit_bytes=56 << 20),
        cost_estimate=pl.CostEstimate(flops=4_000_000_000, bytes_accessed=9_000_000, transcendentals=1_000_000),
        name="first_rows",
    )(flags, x, tail, w_query, w_key, w_value, w_out, g1, g2, conv_weight, q0, k0, v0, hid0, cin0, out)
    return out[None]


def solution(mesh):
    in_specs = (P("rec", "tm", None), P("rec", None, None), P(), P(), P(), P(), P(), P(), P())
    out_specs = P("rec", "tm", None)
    return jax.shard_map(
        per_device, mesh=mesh, in_specs=in_specs, out_specs=out_specs, check_vma=False
    )
```

time: 364 us -> 88.5 us (0.24)
  the two profiles are of different devices: /device:TPU:16 before, /device:TPU:1 now
where the time goes in v1:
time: 88.5 us; the launch traced here: 87.6 us
  Pallas kernels  76.8 us (87%)
  local copies, waits for them, and re-layouts  5.36 us (6%)
  starting transfers between devices  4.42 us (5%)
    pallas_call x1, Pallas kernels, per_device(): pl.pallas_call(kernel_a, in_specs=[smem, hbm, hbm, hbm, hbm, hbm, vmem, v...  56.1 us
    pallas_call x1, Pallas kernels, per_device(): pl.pallas_call(kernel_b, in_specs=[smem, hbm, vmem, hbm, hbm, hbm, hbm] +...  20.7 us
    ppermute x1, starting transfers between devices, per_device(): lax.ppermute(x[count - EXTRA:], 'tm', [(i, i + 1) for i in range(peers -...  4.42 us
  transfers between devices with their start and end apart: 1, of which 0 were waited for; matrix products, arithmetic and copies ran while one was open for 5% of the time, Pallas kernels for 64%

profile of v1, /device:TPU:1, one launch (start us, length us, event | category | flops | bytes accessed | tf_op | source)
XLA Modules:
  0.0 87.6 jit_solution(16713404470619233847)
XLA Ops:
  0.0 1.2 %slice_bitcast_fusion = bf16[288,1280]{1,0:T(8,128)(2,1)S(1)} fusion(bf16[1,1024,1280]{2,1,0:T(8,128)(2,1)} %param.9), kind=kLoop, calls=%fused_computation | loop fusion | bytes 1474560 | tf_op jit(solution)/shard_map/slice | solution.py:242
  1.2 4.4 %collective-permute-start = (bf16[288,1280]{1,0:T(8,128)(2,1)S(1)}, bf16[288,1280]{1,0:T(8,128)(2,1)S(1)}, u32[]{:S(2)}, u32[]{:S(2)}) collective-permute-start(bf16[288,1280]{1,0:T(8,128)(2,1)S(1)} %slice_bitcast_fusion), channel_id=1, source_target_pairs={{0,1},{1,2},{2,3},{3,4},{4,5},{5,6},{6,7},{7,8},{8,9},{9,10},{10,1... | collective-permute-start | bytes 2211848 | tf_op jit(solution)/shard_map/ppermute | solution.py:242
  5.6 0.8 fusion
  6.4 0.2 and_reduce_fusion
  6.6 1.3 %reshape.19.g1 = f32[1,1280]{1,0:T(1,128)} reshape(f32[1280]{0:T(1024)} %param.11) | data formatting | bytes 10240 | tf_op jit(solution)/shard_map/reshape | solution.py:246
  7.9 1.3 %reshape.20.g2 = f32[1,1280]{1,0:T(1,128)} reshape(f32[1280]{0:T(1024)} %param.16) | data formatting | bytes 10240 | tf_op jit(solution)/shard_map/reshape | solution.py:247
  9.2 0.6 pad_add_fusion.flags
  9.8 56.1 %own_rows.1 = (bf16[1024,1280]{1,0:T(8,128)(2,1)}, bf16[256,640]{1,0:T(8,128)(2,1)}, bf16[256,640]{1,0:T(8,128)(2,1)}, bf16[256,640]{1,0:T(8,128)(2,1)}, f32[32,1280]{1,0:T(8,128)}, /*index=5*/f32[10,32,128]{2,1,0:T(8,128)}) custom-call(s32[12]{0:T(128)} %pad_add_fusion.flags, bf16[1024,1280]{1,0:T(8,128)(2,1)} %bitcast.8, bf16[1280,640]{1,0:T(8,128)(2,1)} %wq_hbm.3, ...), custom_call_target="tpu_custom_call" | custom-call | flops 12000000000 | bytes 11000000 | tf_op jit(solution)/shard_map/own_rows/pallas_call | solution.py:252
  65.9 0.0 collective-permute-done.tail
  65.9 0.0 copy-start
  65.9 0.9 copy-done
  66.8 20.7 %first_rows.1 = bf16[1024,1280]{1,0:T(8,128)(2,1)} custom-call(s32[12]{0:T(128)} %pad_add_fusion.flags, bf16[1024,1280]{1,0:T(8,128)(2,1)} %bitcast.9, bf16[288,1280]{1,0:T(8,128)(2,1)} %copy-done, bf16[1280,640]{1,0:T(8,128)(2,1)} %wq_hbm.3, bf16[1280,640]{1,0:T(8,128)(2,1)} %wk_hbm.3, bf16[1280,640]{1,0:T(8,128)(2,1)} %wv_hbm.3, ...), custom_call_target="tpu_custom_call", output_to_operand_aliasing={{}: (15, {})} | custom-call | flops 4000000000 | bytes 9000000 | tf_op jit(solution)/shard_map/first_rows/pallas_call | solution.py:283
  (2 shorter events, 0.0 us)
Async XLA Ops:
  1.2 64.8 %collective-permute-start = (bf16[288,1280]{1,0:T(8,128)(2,1)S(1)}, bf16[288,1280]{1,0:T(8,128)(2,1)S(1)}, u32[]{:S(2)}, u32[]{:S(2)}) collective-permute-start(bf16[288,1280]{1,0:T(8,128)(2,1)S(1)} %slice_bitcast_fusion), channel_id=1, source_target_pairs={{0,1},{1,2},{2,3},{3,4},{4,5},{5,6},{6,7},{7,8},{8,9},{9,10},{10,1... | collective-permute-start | bytes 2211848 | tf_op jit(solution)/shard_map/ppermute | solution.py:242
  65.9 0.9 copy-start

commit v2 on v1

v2 whole, which is shorter than its diff:
```python
import jax
import jax.experimental.pallas as pl
import jax.experimental.pallas.tpu as pltpu
import jax.numpy as jnp
from jax import lax
from jax.sharding import PartitionSpec as P

H = 10
HS = 64
CTX = 256
KSZ = 31
ROWS = 256
HALO = 32
EXTRA = CTX + HALO
SEGS = 256
SPLIT = 480
LANES = 128
SCALE = 0.125 * 1.4426950408889634
NEG = -1e30


def lane_sum(v):
    total = v[:, :LANES]
    for t in range(1, v.shape[1] // LANES):
        total = total + v[:, t * LANES : (t + 1) * LANES]
    return jnp.sum(total, axis=-1, keepdims=True) * (1.0 / v.shape[1])


def norm_staged(load, store, count, gain, step=16):
    means, scales = [], []
    for r in range(0, count, step):
        means.append(lane_sum(load(r, True)))
    for mean, r in zip(means, range(0, count, step)):
        centred = load(r, False) - mean
        scales.append(lax.rsqrt(lane_sum(centred * centred) + 1e-05))
    for mean, scale, r in zip(means, scales, range(0, count, step)):
        store(r, (load(r, False) - mean) * scale * gain)


def norm_rows(src, dst, first, count, gain, step=16):
    def load(r, _):
        return src[pl.ds(pl.multiple_of(first + r, 16), step), :].astype(jnp.float32)

    def store(r, value):
        dst[pl.ds(pl.multiple_of(first + r, 16), step), :] = value.astype(jnp.bfloat16)

    norm_staged(load, store, count, gain, step)


def tri_masks(rows):
    i = lax.broadcasted_iota(jnp.int32, (rows, ROWS), 0)
    j = lax.broadcasted_iota(jnp.int32, (rows, ROWS), 1)
    return j <= i


def bias_row(flags, marks):
    lane = lax.broadcasted_iota(jnp.int32, (1, ROWS), 1)
    row = jnp.full((1, ROWS), NEG, jnp.float32)
    for upto, flag in reversed(marks):
        row = jnp.where(lane < upto, jnp.where(flags[flag] > 0, 0.0, NEG), row)
    return row


def attend(q_ref, q_first, k_ref, v_ref, prev_first, rows, bias, tri, heads_ref, out_first):
    cur_first = prev_first + ROWS
    lane = lax.broadcasted_iota(jnp.int32, (rows, LANES), 1)
    tri01 = jnp.where(tri, 1.0, 0.0).astype(jnp.bfloat16)
    ones = jnp.ones((ROWS, LANES), jnp.bfloat16)
    zero = jnp.zeros((rows, LANES), jnp.bfloat16)
    for pair in range(H // 2):
        cols = slice(pair * LANES, (pair + 1) * LANES)
        q = q_ref[pl.ds(q_first, rows), cols]
        kp = k_ref[pl.ds(prev_first, ROWS), cols]
        kc = k_ref[pl.ds(cur_first, ROWS), cols]
        vp = jnp.concatenate([v_ref[pl.ds(prev_first, ROWS), cols], ones], axis=1)
        vc = jnp.concatenate([v_ref[pl.ds(cur_first, ROWS), cols], ones], axis=1)
        outs = []
        for half in range(2):
            mine = (lane < HS) if half == 0 else (lane >= HS)
            qh = jnp.where(mine, q, zero)
            dims = (((1,), (1,)), ((), ()))
            sp = lax.dot_general(qh, kp, dims, preferred_element_type=jnp.float32)
            sc = lax.dot_general(qh, kc, dims, preferred_element_type=jnp.float32)
            s = jnp.where(tri, sc, sp) + bias
            top = jnp.max(s, axis=-1, keepdims=True)
            p = jnp.exp2((s - top) * SCALE).astype(jnp.bfloat16)
            pc = p * tri01
            pp = p - pc
            outs.append(
                jnp.dot(pp, vp, preferred_element_type=jnp.float32)
                + jnp.dot(pc, vc, preferred_element_type=jnp.float32)
            )
        first = lane < HS
        num = jnp.where(first, outs[0][:, :LANES], outs[1][:, :LANES])
        den = jnp.where(first, outs[0][:, LANES:], outs[1][:, LANES:])
        heads_ref[pl.ds(out_first, rows), cols] = (num / den).astype(jnp.bfloat16)


def fir_weights(w_ref, cols):
    def add(a, b):
        return a if b is None else a + b

    w = [w_ref[pl.ds(j, 1), cols] for j in range(KSZ)] + [None]
    even, odd = w[0::2], w[1::2]
    sets = []
    for h in (even, odd, [add(a, b) for a, b in zip(even, odd)]):
        first, second = h[0::2], h[1::2]
        sets += [first, second, [add(a, b) for a, b in zip(first, second)]]
    return [[None if t is None else jnp.broadcast_to(t, (8, LANES)) for t in h] for h in sets]


def conv_seg(cbuf, w_ref, c, cols, base, units, comb, part, ybuf):
    seg = 4 * units
    weights = fir_weights(w_ref, cols)
    for u in range(-8, units):
        x = [cbuf[c, pl.ds(base + HALO + 4 * u + p, 8, stride=seg), :] for p in range(4)]
        low, high = x[0] + x[1], x[2] + x[3]
        for f, t in enumerate((x[0], x[2], x[0] + x[2], x[1], x[3], x[1] + x[3], low, high, low + high)):
            comb[f, u + 8] = t
    for f, h in enumerate(weights):
        lo = 0 if f in (0, 2, 6, 8) else -1
        xs = {u: comb[f, u + 8] for u in range(lo - 7, units)}
        for u in range(lo, units):
            acc = None
            for m in range(8):
                if h[m] is not None:
                    t = h[m] * xs[u - m]
                    acc = t if acc is None else acc + t
            part[f, u + 1] = acc
    b1, b4, b7 = part[1, 0], part[4, 0], part[7, 0]
    before = part[5, 0] - (part[3, 0] + b4)
    for u in range(units):
        b = [part[f, u + 1] for f in range(9)]
        a1e, a1o = b[0] + b1, b[2] - (b[0] + b[1])
        a2e, a2o = b[3] + b4, b[5] - (b[3] + b[4])
        a3e, a3o = b[6] + b7, b[8] - (b[6] + b[7])
        y = (a1e + before, a3e - (a1e + a2e), a1o + a2e, a3o - (a1o + a2o))
        b1, b4, b7, before = b[1], b[4], b[7], a2o
        for p in range(4):
            ybuf[pl.ds(4 * u + p, 8, stride=seg), :] = y[p]


def residual(x_ref, x_first, attn_ref, flags, marks, hid_ref, hid_first, cbuf, cbuf_first, gain, scale=None):
    def load(r, first):
        if not first:
            return hid_ref[pl.ds(hid_first + r, 16), :]
        on = [flags[flag] for upto, flag in reversed(marks) if r < upto][-1] > 0
        xf = x_ref[pl.ds(x_first + r, 16), :].astype(jnp.float32)
        hidden = jnp.where(on, xf + attn_ref[pl.ds(r, 16), :], xf)
        hid_ref[pl.ds(hid_first + r, 16), :] = hidden
        return hidden

    def store(r, value):
        value = value.astype(jnp.bfloat16).astype(jnp.float32)
        if scale is not None:
            value = value * scale
        for c in range(10):
            cbuf[c, pl.ds(cbuf_first + r, 16), :] = value[:, c * LANES : (c + 1) * LANES]

    norm_staged(load, store, marks[-1][0], gain)


def conv_rows(cbuf, w_ref, hid_ref, flags, first, units, comb, part, ybuf, out_ref, out_hbm, sems):
    count = 32 * units

    def lanes(c, carry):
        cols = pl.ds(pl.multiple_of(c * LANES, LANES), LANES)
        conv_seg(cbuf, w_ref, c, cols, first, units, comb, part, ybuf)
        for r in range(0, count, 32):
            on = flags[3 + (first + r) // LANES] > 0
            half = ybuf[pl.ds(r, 32), :] * 0.5
            hidden = hid_ref[pl.ds(first + r, 32), cols]
            out = jnp.where(on, hidden + (half + half * jnp.tanh(half)), hidden)
            out_ref[pl.ds(r, 32), cols] = out.astype(jnp.bfloat16)
        send(c).start()
        return carry

    def send(c):
        cols = pl.ds(pl.multiple_of(c * LANES, LANES), LANES)
        return pltpu.make_async_copy(
            out_ref.at[:, cols], out_hbm.at[pl.ds(first, count), cols], sems.at[c]
        )

    def finish(c, carry):
        send(c).wait()
        return carry

    lax.fori_loop(0, 10, lanes, 0)
    lax.fori_loop(0, 10, finish, 0)


def block_flags(segs, base):
    times = [base + (i - 3) * LANES for i in range(11)]
    lows = [jnp.int32(0)] * 11
    step = SEGS // 2
    while step:
        lows = [jnp.where(segs[2 * (lo + step)] <= t, lo + step, lo) for lo, t in zip(lows, times)]
        step //= 2
    return [
        ((t >= 0) & (segs[2 * lo] <= t) & (t < segs[2 * lo + 1])).astype(jnp.int32) for lo, t in zip(lows, times)
    ]


def kernel_a(segs, place, x_hbm, wq_hbm, wk_hbm, wv_hbm, wo_hbm, g1, g2, cw, out_hbm, q0, k0, v0, hid0, cin0, flags0,
             x, wqkv, wo, normed, q, k, v, heads, attn, hid, cbuf, out, comb, part, ybuf, sems, out_sems):
    feats = H * HS
    copies = [
        pltpu.make_async_copy(x_hbm, x, sems.at[0]),
        pltpu.make_async_copy(wq_hbm, wqkv.at[:, pl.ds(0, feats)], sems.at[1]),
        pltpu.make_async_copy(wk_hbm, wqkv.at[:, pl.ds(feats, feats)], sems.at[2]),
        pltpu.make_async_copy(wv_hbm, wqkv.at[:, pl.ds(2 * feats, feats)], sems.at[3]),
        pltpu.make_async_copy(wo_hbm, wo, sems.at[4]),
    ]
    for copy in copies:
        copy.start()
    flags = block_flags(segs, place[0])
    for i in range(11):
        flags0[i] = flags[i]
    flags0[11] = jnp.minimum(place[0], 1)
    gain1 = g1[...].reshape(1, -1)
    gain2 = g2[...].reshape(1, -1)
    copies[0].wait()
    for b in range(4):
        norm_rows(x, normed, b * ROWS, ROWS, gain1)
    for copy in copies[1:]:
        copy.wait()
    for b in range(4):
        rows = pl.ds(b * ROWS, ROWS)
        for part_at, dst in enumerate((q, k, v)):
            dst[rows, :] = jnp.dot(
                normed[rows, :], wqkv[:, part_at * feats : (part_at + 1) * feats], preferred_element_type=jnp.float32
            ).astype(jnp.bfloat16)
    first = [pltpu.make_async_copy(src.at[pl.ds(0, ROWS), :], dst, sems.at[i]) for i, (src, dst) in enumerate(((q, q0), (k, k0), (v, v0)))]
    for copy in first:
        copy.start()
    tri = tri_masks(ROWS)
    for b in range(1, 4):
        f = 3 + 2 * b
        bias = jnp.where(
            tri,
            bias_row(flags, [(128, f), (256, f + 1)]),
            bias_row(flags, [(128, f - 2), (256, f - 1)]),
        )
        attend(q, b * ROWS, k, v, (b - 1) * ROWS, ROWS, bias, tri, heads, 0)
        attn[...] = jnp.dot(heads[...], wo[...], preferred_element_type=jnp.float32)
        residual(x, b * ROWS, attn, flags, [(128, f), (256, f + 1)], hid, b * ROWS, cbuf, HALO + b * ROWS, gain2)
    rest = [
        pltpu.make_async_copy(hid.at[pl.ds(ROWS, SPLIT - ROWS), :], hid0, sems.at[3]),
        pltpu.make_async_copy(cbuf.at[:, pl.ds(HALO + ROWS, SPLIT - ROWS), :], cin0, sems.at[4]),
    ]
    for copy in rest:
        copy.start()
    conv_rows(cbuf, cw, hid, flags, SPLIT, (1024 - SPLIT) // 32, comb, part, ybuf, out, out_hbm, out_sems)
    for copy in first + rest:
        copy.wait()


def kernel_b(flags, x_hbm, tail_hbm, wq_hbm, wk_hbm, wv_hbm, wo_hbm, g1, g2, cw, q0, k0, v0, hid0, cin0, _, out_hbm,
             tail, x, wqkv, wo, normed, q, k, v, heads, attn, hid, halo_hid, cbuf, out, comb, part, ybuf, sems, out_sems):
    feats = H * HS
    copies = [
        pltpu.make_async_copy(tail_hbm, tail, sems.at[0]),
        pltpu.make_async_copy(wq_hbm, wqkv.at[:, pl.ds(0, feats)], sems.at[1]),
        pltpu.make_async_copy(wk_hbm, wqkv.at[:, pl.ds(feats, feats)], sems.at[2]),
        pltpu.make_async_copy(wv_hbm, wqkv.at[:, pl.ds(2 * feats, feats)], sems.at[3]),
        pltpu.make_async_copy(q0, q.at[pl.ds(HALO, ROWS), :], sems.at[4]),
        pltpu.make_async_copy(k0, k.at[pl.ds(EXTRA, ROWS), :], sems.at[5]),
        pltpu.make_async_copy(v0, v.at[pl.ds(EXTRA, ROWS), :], sems.at[6]),
        pltpu.make_async_copy(wo_hbm, wo, sems.at[7]),
        pltpu.make_async_copy(x_hbm.at[pl.ds(0, ROWS), :], x, sems.at[8]),
        pltpu.make_async_copy(hid0, hid.at[pl.ds(ROWS, SPLIT - ROWS), :], sems.at[9]),
        pltpu.make_async_copy(cin0, cbuf.at[:, pl.ds(HALO + ROWS, SPLIT - ROWS), :], sems.at[10]),
    ]
    for copy in copies:
        copy.start()
    gain1 = g1[...].reshape(1, -1)
    gain2 = g2[...].reshape(1, -1)
    copies[0].wait()
    norm_rows(tail, normed, 0, EXTRA, gain1)
    for copy in copies[1:7]:
        copy.wait()
    q[pl.ds(0, HALO), :] = jnp.dot(
        normed[pl.ds(CTX, HALO), :], wqkv[:, :feats], preferred_element_type=jnp.float32
    ).astype(jnp.bfloat16)
    for part_at, dst in ((1, k), (2, v)):
        dst[pl.ds(0, EXTRA), :] = jnp.dot(
            normed[...], wqkv[:, part_at * feats : (part_at + 1) * feats], preferred_element_type=jnp.float32
        ).astype(jnp.bfloat16)
    small = tri_masks(HALO)
    bias = jnp.where(
        small, bias_row(flags, [(HALO, 2)]), bias_row(flags, [(HALO, 0), (HALO + 128, 1), (256, 2)])
    )
    attend(q, 0, k, v, 0, HALO, bias, small, heads, 0)
    tri = tri_masks(ROWS)
    bias = jnp.where(
        tri, bias_row(flags, [(128, 3), (256, 4)]), bias_row(flags, [(128, 1), (256, 2)])
    )
    attend(q, HALO, k, v, HALO, ROWS, bias, tri, heads, HALO)
    for copy in copies[7:]:
        copy.wait()
    attn[...] = jnp.dot(heads[...], wo[...], preferred_element_type=jnp.float32)
    keep = jnp.where(flags[11] > 0, 1.0, 0.0)
    residual(tail, CTX, attn, flags, [(HALO, 2)], halo_hid, 0, cbuf, 0, gain2, keep)
    residual(x, 0, attn.at[pl.ds(HALO, ROWS), :], flags, [(128, 3), (256, 4)], hid, 0, cbuf, HALO, gain2)
    conv_rows(cbuf, cw, hid, flags, 0, SPLIT // 32, comb, part, ybuf, out, out_hbm, out_sems)


def per_device(frames, segments, ln_gain, w_query, w_key, w_value, w_out, conv_gain, conv_weight):
    x = frames[0]
    count, width = x.shape
    feats = H * HS
    peers = lax.axis_size("tm")
    me = lax.axis_index("tm")
    tail = lax.ppermute(x[count - EXTRA :], "tm", [(i, i + 1) for i in range(peers - 1)])
    place = (me * count).reshape(1).astype(jnp.int32)
    segs = segments.reshape(2 * SEGS)
    hbm = pl.BlockSpec(memory_space=pl.ANY)
    vmem = pl.BlockSpec(memory_space=pltpu.VMEM)
    smem = pl.BlockSpec(memory_space=pltpu.SMEM)
    bf16, f32 = jnp.bfloat16, jnp.float32
    late = count - SPLIT
    out, q0, k0, v0, hid0, cin0, flags = pl.pallas_call(
        kernel_a,
        in_specs=[smem, smem, hbm, hbm, hbm, hbm, hbm, vmem, vmem, vmem],
        out_specs=[hbm] * 6 + [smem],
        out_shape=[
            jax.ShapeDtypeStruct((count, width), bf16),
            jax.ShapeDtypeStruct((ROWS, feats), bf16),
            jax.ShapeDtypeStruct((ROWS, feats), bf16),
            jax.ShapeDtypeStruct((ROWS, feats), bf16),
            jax.ShapeDtypeStruct((SPLIT - ROWS, width), f32),
            jax.ShapeDtypeStruct((10, SPLIT - ROWS, LANES), f32),
            jax.ShapeDtypeStruct((12,), jnp.int32),
        ],
        scratch_shapes=[
            pltpu.VMEM((count, width), bf16),
            pltpu.VMEM((width, 3 * feats), bf16),
            pltpu.VMEM((feats, width), bf16),
            pltpu.VMEM((count, width), bf16),
            pltpu.VMEM((count, feats), bf16),
            pltpu.VMEM((count, feats), bf16),
            pltpu.VMEM((count, feats), bf16),
            pltpu.VMEM((ROWS, feats), bf16),
            pltpu.VMEM((ROWS, width), f32),
            pltpu.VMEM((count, width), f32),
            pltpu.VMEM((10, HALO + count, LANES), f32),
            pltpu.VMEM((late, width), bf16),
            pltpu.VMEM((9, late // 32 + 8, 8, LANES), f32),
            pltpu.VMEM((9, late // 32 + 1, 8, LANES), f32),
            pltpu.VMEM((late, LANES), f32),
            pltpu.SemaphoreType.DMA((5,)),
            pltpu.SemaphoreType.DMA((10,)),
        ],
        compiler_params=pltpu.CompilerParams(vmem_limit_bytes=56 << 20),
        cost_estimate=pl.CostEstimate(flops=12_000_000_000, bytes_accessed=11_000_000, transcendentals=4_000_000),
        name="own_rows",
    )(segs, place, x, w_query, w_key, w_value, w_out, ln_gain, conv_gain, conv_weight)
    out = pl.pallas_call(
        kernel_b,
        in_specs=[smem] + [hbm] * 6 + [vmem] * 3 + [hbm] * 6,
        out_specs=hbm,
        out_shape=jax.ShapeDtypeStruct((count, width), bf16),
        input_output_aliases={15: 0},
        scratch_shapes=[
            pltpu.VMEM((EXTRA, width), bf16),
            pltpu.VMEM((ROWS, width), bf16),
            pltpu.VMEM((width, 3 * feats), bf16),
            pltpu.VMEM((feats, width), bf16),
            pltpu.VMEM((EXTRA, width), bf16),
            pltpu.VMEM((EXTRA, feats), bf16),
            pltpu.VMEM((EXTRA + ROWS, feats), bf16),
            pltpu.VMEM((EXTRA + ROWS, feats), bf16),
            pltpu.VMEM((EXTRA, feats), bf16),
            pltpu.VMEM((EXTRA, width), f32),
            pltpu.VMEM((SPLIT, width), f32),
            pltpu.VMEM((HALO, width), f32),
            pltpu.VMEM((10, HALO + SPLIT, LANES), f32),
            pltpu.VMEM((SPLIT, width), bf16),
            pltpu.VMEM((9, SPLIT // 32 + 8, 8, LANES), f32),
            pltpu.VMEM((9, SPLIT // 32 + 1, 8, LANES), f32),
            pltpu.VMEM((SPLIT, LANES), f32),
            pltpu.SemaphoreType.DMA((11,)),
            pltpu.SemaphoreType.DMA((10,)),
        ],
        compiler_params=pltpu.CompilerParams(vmem_limit_bytes=56 << 20),
        cost_estimate=pl.CostEstimate(flops=4_000_000_000, bytes_accessed=9_000_000, transcendentals=1_000_000),
        name="first_rows",
    )(flags, x, tail, w_query, w_key, w_value, w_out, ln_gain, conv_gain, conv_weight, q0, k0, v0, hid0, cin0, out)
    return out[None]


def solution(mesh):
    in_specs = (P("rec", "tm", None), P("rec", None, None), P(), P(), P(), P(), P(), P(), P())
    out_specs = P("rec", "tm", None)
    return jax.shard_map(
        per_device, mesh=mesh, in_specs=in_specs, out_specs=out_specs, check_vma=False
    )
```

time: 88.5 us -> 47.9 us (0.54)
  Pallas kernels: 76.8 us -> 38.8 us
  local copies, waits for them, and re-layouts: 5.36 us -> 3.57 us
    pallas_call x2, Pallas kernels: 76.8 us -> 38.8 us  [the longest x1 24.5 us: per_device(): pl.pallas_call(kernel_a, in_specs=[smem, smem, hbm, hbm, hbm, hbm, hbm, v...]
    reshape x2 -> x1, local copies, waits for them, and re-layouts: 2.58 us -> 0.74 us  [per_device(): segs = segments.reshape(2 * SEGS)]
  transfers between devices with their start and end apart: 1 -> 1, of which waited for: 0 -> 0; matrix products, arithmetic and copies ran while one was open for 5% -> 3% of each run, Pallas kernels for 64% -> 52%
where the time goes in v2:
time: 47.9 us; the launch traced here: 47 us
  Pallas kernels  38.8 us (81%)
  starting transfers between devices  4.42 us (9%)
  local copies, waits for them, and re-layouts  3.57 us (7%)
    pallas_call x1, Pallas kernels, per_device(): pl.pallas_call(kernel_a, in_specs=[smem, smem, hbm, hbm, hbm, hbm, hbm, v...  24.5 us
    pallas_call x1, Pallas kernels, per_device(): pl.pallas_call(kernel_b, in_specs=[smem] + [hbm] * 6 + [vmem] * 3 + [hbm]...  14.3 us
    ppermute x1, starting transfers between devices, per_device(): lax.ppermute(x[count - EXTRA:], 'tm', [(i, i + 1) for i in range(peers -...  4.42 us
    unnamed x3, local copies, waits for them, and re-layouts  1.67 us
    slice x1, local copies, waits for them, and re-layouts, per_device(): x[count - EXTRA:]  1.16 us
  transfers between devices with their start and end apart: 1, of which 0 were waited for; matrix products, arithmetic and copies ran while one was open for 3% of the time, Pallas kernels for 52%

profile of v2, /device:TPU:1, one launch (start us, length us, event | category | flops | bytes accessed | tf_op | source)
XLA Modules:
  0.0 47.0 jit_solution(15469430935750488039)
XLA Ops:
  0.0 1.2 %slice_bitcast_fusion = bf16[288,1280]{1,0:T(8,128)(2,1)S(1)} fusion(bf16[1,1024,1280]{2,1,0:T(8,128)(2,1)} %param.9), kind=kLoop, calls=%fused_computation | loop fusion | bytes 1474560 | tf_op jit(solution)/shard_map/slice | solution.py:314
  1.2 4.4 %collective-permute-start = (bf16[288,1280]{1,0:T(8,128)(2,1)S(1)}, bf16[288,1280]{1,0:T(8,128)(2,1)S(1)}, u32[]{:S(2)}, u32[]{:S(2)}) collective-permute-start(bf16[288,1280]{1,0:T(8,128)(2,1)S(1)} %slice_bitcast_fusion), channel_id=1, source_target_pairs={{0,1},{1,2},{2,3},{3,4},{4,5},{5,6},{6,7},{7,8},{8,9},{9,10},{10,1... | collective-permute-start | bytes 2211848 | tf_op jit(solution)/shard_map/ppermute | solution.py:314
  5.6 0.8 %copy.11 = s32[1,256,2]{2,1,0:T(8,128)S(1)} copy(s32[1,256,2]{1,2,0:T(2,128)} %param.10) | data formatting | bytes 4096 | tf_op args[1]
  6.4 0.7 %reshape.7.segs = s32[512]{0:T(512)} reshape(s32[1,256,2]{2,1,0:T(8,128)S(1)} %copy.11) | data formatting | bytes 4096 | tf_op jit(solution)/shard_map/reshape | solution.py:316
  7.2 24.5 %own_rows.1 = (bf16[1024,1280]{1,0:T(8,128)(2,1)}, bf16[256,640]{1,0:T(8,128)(2,1)}, bf16[256,640]{1,0:T(8,128)(2,1)}, bf16[256,640]{1,0:T(8,128)(2,1)}, f32[224...) custom-call(s32[512]{0:T(512)} %reshape.7.segs, s32[1]{0:T(128)} %bitcast.place, bf16[1024,1280]{1,0:T(8,128)(2,1)} %bitcast.5, ...), custom_call_target="tpu_custom_call" | custom-call | flops 12000000000 | bytes 11000000 | tf_op jit(solution)/shard_map/own_rows/pallas_call | solution.py:322
  31.7 0.0 collective-permute-done.tail_hbm
  31.7 0.0 copy-start
  31.7 0.9 %copy-done = bf16[288,1280]{1,0:T(8,128)(2,1)} copy-done((bf16[288,1280]{1,0:T(8,128)(2,1)}, bf16[288,1280]{1,0:T(8,128)(2,1)S(1)}, u32[]{:S(2)}) %copy-start) | copy-done | bytes 737304
  32.6 14.3 %first_rows.1 = bf16[1024,1280]{1,0:T(8,128)(2,1)} custom-call(s32[12]{0:T(128)} %get-tuple-element.12.flags, bf16[1024,1280]{1,0:T(8,128)(2,1)} %bitcast.6, bf16[288,1280]{1,0:T(8,128)(2,1)} %copy-done, bf16[1280,640]{1,0:T(8,128)(2,1)} %wq_hbm.3, bf16[1280,640]{1,0:T(8,128)(2,1)} %wk_hbm.3, ...), custom_call_target="tpu_custom_call", output_to_operand_aliasing={{}: (15, {})} | custom-call | flops 4000000000 | bytes 9000000 | tf_op jit(solution)/shard_map/first_rows/pallas_call | solution.py:358
Async XLA Ops:
  1.2 30.5 %collective-permute-start = (bf16[288,1280]{1,0:T(8,128)(2,1)S(1)}, bf16[288,1280]{1,0:T(8,128)(2,1)S(1)}, u32[]{:S(2)}, u32[]{:S(2)}) collective-permute-start(bf16[288,1280]{1,0:T(8,128)(2,1)S(1)} %slice_bitcast_fusion), channel_id=1, source_target_pairs={{0,1},{1,2},{2,3},{3,4},{4,5},{5,6},{6,7},{7,8},{8,9},{9,10},{10,1... | collective-permute-start | bytes 2211848 | tf_op jit(solution)/shard_map/ppermute | solution.py:314
  31.7 0.9 %copy-start = (bf16[288,1280]{1,0:T(8,128)(2,1)}, bf16[288,1280]{1,0:T(8,128)(2,1)S(1)}, u32[]{:S(2)}) copy-start(bf16[288,1280]{1,0:T(8,128)(2,1)S(1)} %collective-permute-done.tail_hbm) | copy-start | bytes 2211844

commit v3 on v2

--- a/solution.py
+++ b/solution.py
@@ -194,43 +194,55 @@
     lows = [jnp.int32(0)] * 11
     step = SEGS // 2
     while step:
-        lows = [jnp.where(segs[2 * (lo + step)] <= t, lo + step, lo) for lo, t in zip(lows, times)]
+        lows = [jnp.where(segs[0, lo + step] <= t, lo + step, lo) for lo, t in zip(lows, times)]
         step //= 2
     return [
-        ((t >= 0) & (segs[2 * lo] <= t) & (t < segs[2 * lo + 1])).astype(jnp.int32) for lo, t in zip(lows, times)
+        ((t >= 0) & (segs[0, lo] <= t) & (t < segs[1, lo])).astype(jnp.int32) for lo, t in zip(lows, times)
     ]
 
 
-def kernel_a(segs, place, x_hbm, wq_hbm, wk_hbm, wv_hbm, wo_hbm, g1, g2, cw, out_hbm, q0, k0, v0, hid0, cin0, flags0,
-             x, wqkv, wo, normed, q, k, v, heads, attn, hid, cbuf, out, comb, part, ybuf, sems, out_sems):
+def kernel_a(segs, place, x_hbm, wq_hbm, wk_hbm, wv_hbm, wo_hbm, g1, g2, cw, out_hbm, q0, kv0, hid0, cin0, flags0,
+             x, wqkv, wo, normed, qkv, heads, attn, hid, cbuf, out, comb, part, ybuf, sems, out_sems):
     feats = H * HS
+    q, k, v = (qkv.at[:, pl.ds(i * feats, feats)] for i in range(3))
     copies = [
-        pltpu.make_async_copy(x_hbm, x, sems.at[0]),
-        pltpu.make_async_copy(wq_hbm, wqkv.at[:, pl.ds(0, feats)], sems.at[1]),
-        pltpu.make_async_copy(wk_hbm, wqkv.at[:, pl.ds(feats, feats)], sems.at[2]),
-        pltpu.make_async_copy(wv_hbm, wqkv.at[:, pl.ds(2 * feats, feats)], sems.at[3]),
-        pltpu.make_async_copy(wo_hbm, wo, sems.at[4]),
+        pltpu.make_async_copy(x_hbm.at[pl.ds(b * ROWS, ROWS), :], x.at[pl.ds(b * ROWS, ROWS), :], sems.at[b])
+        for b in range(4)
+    ] + [
+        pltpu.make_async_copy(wq_hbm, wqkv.at[:, pl.ds(0, feats)], sems.at[4]),
+        pltpu.make_async_copy(wk_hbm, wqkv.at[:, pl.ds(feats, feats)], sems.at[5]),
+        pltpu.make_async_copy(wv_hbm, wqkv.at[:, pl.ds(2 * feats, feats)], sems.at[6]),
+        pltpu.make_async_copy(wo_hbm, wo, sems.at[7]),
     ]
-    for copy in copies:
-        copy.start()
+    for i in (0, 4, 1, 2, 3, 5, 6, 7):
+        copies[i].start()
     flags = block_flags(segs, place[0])
     for i in range(11):
         flags0[i] = flags[i]
     flags0[11] = jnp.minimum(place[0], 1)
     gain1 = g1[...].reshape(1, -1)
     gain2 = g2[...].reshape(1, -1)
-    copies[0].wait()
+    def project(b, lo, hi):
+        rows = pl.ds(b * ROWS, ROWS)
+        qkv[rows, lo:hi] = jnp.dot(
+            normed[rows, :], wqkv[:, lo:hi], preferred_element_type=jnp.float32
+        ).astype(jnp.bfloat16)
+
     for b in range(4):
+        copies[b].wait()
         norm_rows(x, normed, b * ROWS, ROWS, gain1)
-    for copy in copies[1:]:
-        copy.wait()
-    for b in range(4):
-        rows = pl.ds(b * ROWS, ROWS)
-        for part_at, dst in enumerate((q, k, v)):
-            dst[rows, :] = jnp.dot(
-                normed[rows, :], wqkv[:, part_at * feats : (part_at + 1) * feats], preferred_element_type=jnp.float32
-            ).astype(jnp.bfloat16)
-    first = [pltpu.make_async_copy(src.at[pl.ds(0, ROWS), :], dst, sems.at[i]) for i, (src, dst) in enumerate(((q, q0), (k, k0), (v, v0)))]
+        if b == 0:
+            copies[4].wait()
+        project(b, 0, 512)
+    for i, lo, hi in ((5, 512, 2 * feats), (6, 2 * feats, 3 * feats)):
+        copies[i].wait()
+        for b in range(4):
+            project(b, lo, hi)
+    copies[7].wait()
+    first = [
+        pltpu.make_async_copy(qkv.at[pl.ds(0, ROWS), pl.ds(0, feats)], q0, sems.at[0]),
+        pltpu.make_async_copy(qkv.at[pl.ds(0, ROWS), pl.ds(feats, 2 * feats)], kv0, sems.at[1]),
+    ]
     for copy in first:
         copy.start()
     tri = tri_masks(ROWS)
@@ -241,9 +253,11 @@
             bias_row(flags, [(128, f), (256, f + 1)]),
             bias_row(flags, [(128, f - 2), (256, f - 1)]),
         )
-        attend(q, b * ROWS, k, v, (b - 1) * ROWS, ROWS, bias, tri, heads, 0)
-        attn[...] = jnp.dot(heads[...], wo[...], preferred_element_type=jnp.float32)
-        residual(x, b * ROWS, attn, flags, [(128, f), (256, f + 1)], hid, b * ROWS, cbuf, HALO + b * ROWS, gain2)
+        attend(q, b * ROWS, k, v, (b - 1) * ROWS, ROWS, bias, tri, heads, (b - 1) * ROWS)
+    attn[...] = jnp.dot(heads[...], wo[...], preferred_element_type=jnp.float32)
+    for b in range(1, 4):
+        f = 3 + 2 * b
+        residual(x, b * ROWS, attn.at[pl.ds((b - 1) * ROWS, ROWS), :], flags, [(128, f), (256, f + 1)], hid, b * ROWS, cbuf, HALO + b * ROWS, gain2)
     rest = [
         pltpu.make_async_copy(hid.at[pl.ds(ROWS, SPLIT - ROWS), :], hid0, sems.at[3]),
         pltpu.make_async_copy(cbuf.at[:, pl.ds(HALO + ROWS, SPLIT - ROWS), :], cin0, sems.at[4]),
@@ -255,21 +269,21 @@
         copy.wait()
 
 
-def kernel_b(flags, x_hbm, tail_hbm, wq_hbm, wk_hbm, wv_hbm, wo_hbm, g1, g2, cw, q0, k0, v0, hid0, cin0, _, out_hbm,
-             tail, x, wqkv, wo, normed, q, k, v, heads, attn, hid, halo_hid, cbuf, out, comb, part, ybuf, sems, out_sems):
+def kernel_b(flags, x_hbm, tail_hbm, wq_hbm, wk_hbm, wv_hbm, wo_hbm, g1, g2, cw, q0, kv0, hid0, cin0, _, out_hbm,
+             tail, x, wqkv, wo, normed, q, kv, heads, attn, hid, halo_hid, cbuf, out, comb, part, ybuf, sems, out_sems):
     feats = H * HS
+    k, v = (kv.at[:, pl.ds(i * feats, feats)] for i in range(2))
     copies = [
         pltpu.make_async_copy(tail_hbm, tail, sems.at[0]),
-        pltpu.make_async_copy(wq_hbm, wqkv.at[:, pl.ds(0, feats)], sems.at[1]),
-        pltpu.make_async_copy(wk_hbm, wqkv.at[:, pl.ds(feats, feats)], sems.at[2]),
-        pltpu.make_async_copy(wv_hbm, wqkv.at[:, pl.ds(2 * feats, feats)], sems.at[3]),
+        pltpu.make_async_copy(wk_hbm, wqkv.at[:, pl.ds(feats, feats)], sems.at[1]),
+        pltpu.make_async_copy(wv_hbm, wqkv.at[:, pl.ds(2 * feats, feats)], sems.at[2]),
+        pltpu.make_async_copy(wq_hbm, wqkv.at[:, pl.ds(0, feats)], sems.at[3]),
         pltpu.make_async_copy(q0, q.at[pl.ds(HALO, ROWS), :], sems.at[4]),
-        pltpu.make_async_copy(k0, k.at[pl.ds(EXTRA, ROWS), :], sems.at[5]),
-        pltpu.make_async_copy(v0, v.at[pl.ds(EXTRA, ROWS), :], sems.at[6]),
-        pltpu.make_async_copy(wo_hbm, wo, sems.at[7]),
-        pltpu.make_async_copy(x_hbm.at[pl.ds(0, ROWS), :], x, sems.at[8]),
-        pltpu.make_async_copy(hid0, hid.at[pl.ds(ROWS, SPLIT - ROWS), :], sems.at[9]),
-        pltpu.make_async_copy(cin0, cbuf.at[:, pl.ds(HALO + ROWS, SPLIT - ROWS), :], sems.at[10]),
+        pltpu.make_async_copy(kv0, kv.at[pl.ds(EXTRA, ROWS), :], sems.at[5]),
+        pltpu.make_async_copy(wo_hbm, wo, sems.at[6]),
+        pltpu.make_async_copy(x_hbm.at[pl.ds(0, ROWS), :], x, sems.at[7]),
+        pltpu.make_async_copy(hid0, hid.at[pl.ds(ROWS, SPLIT - ROWS), :], sems.at[8]),
+        pltpu.make_async_copy(cin0, cbuf.at[:, pl.ds(HALO + ROWS, SPLIT - ROWS), :], sems.at[9]),
     ]
     for copy in copies:
         copy.start()
@@ -277,15 +291,17 @@
     gain2 = g2[...].reshape(1, -1)
     copies[0].wait()
     norm_rows(tail, normed, 0, EXTRA, gain1)
-    for copy in copies[1:7]:
-        copy.wait()
+    for i, lo, hi in ((1, 0, 512), (2, 512, 2 * feats)):
+        copies[i].wait()
+        kv[pl.ds(0, EXTRA), lo:hi] = jnp.dot(
+            normed[...], wqkv[:, feats + lo : feats + hi], preferred_element_type=jnp.float32
+        ).astype(jnp.bfloat16)
+    copies[3].wait()
     q[pl.ds(0, HALO), :] = jnp.dot(
         normed[pl.ds(CTX, HALO), :], wqkv[:, :feats], preferred_element_type=jnp.float32
     ).astype(jnp.bfloat16)
-    for part_at, dst in ((1, k), (2, v)):
-        dst[pl.ds(0, EXTRA), :] = jnp.dot(
-            normed[...], wqkv[:, part_at * feats : (part_at + 1) * feats], preferred_element_type=jnp.float32
-        ).astype(jnp.bfloat16)
+    copies[4].wait()
+    copies[5].wait()
     small = tri_masks(HALO)
     bias = jnp.where(
         small, bias_row(flags, [(HALO, 2)]), bias_row(flags, [(HALO, 0), (HALO + 128, 1), (256, 2)])
@@ -296,7 +312,7 @@
         tri, bias_row(flags, [(128, 3), (256, 4)]), bias_row(flags, [(128, 1), (256, 2)])
     )
     attend(q, HALO, k, v, HALO, ROWS, bias, tri, heads, HALO)
-    for copy in copies[7:]:
+    for copy in copies[6:]:
         copy.wait()
     attn[...] = jnp.dot(heads[...], wo[...], preferred_element_type=jnp.float32)
     keep = jnp.where(flags[11] > 0, 1.0, 0.0)
@@ -313,21 +329,20 @@
     me = lax.axis_index("tm")
     tail = lax.ppermute(x[count - EXTRA :], "tm", [(i, i + 1) for i in range(peers - 1)])
     place = (me * count).reshape(1).astype(jnp.int32)
-    segs = segments.reshape(2 * SEGS)
+    segs = segments[0].T
     hbm = pl.BlockSpec(memory_space=pl.ANY)
     vmem = pl.BlockSpec(memory_space=pltpu.VMEM)
     smem = pl.BlockSpec(memory_space=pltpu.SMEM)
     bf16, f32 = jnp.bfloat16, jnp.float32
     late = count - SPLIT
-    out, q0, k0, v0, hid0, cin0, flags = pl.pallas_call(
+    out, q0, kv0, hid0, cin0, flags = pl.pallas_call(
         kernel_a,
         in_specs=[smem, smem, hbm, hbm, hbm, hbm, hbm, vmem, vmem, vmem],
-        out_specs=[hbm] * 6 + [smem],
+        out_specs=[hbm] * 5 + [smem],
         out_shape=[
             jax.ShapeDtypeStruct((count, width), bf16),
             jax.ShapeDtypeStruct((ROWS, feats), bf16),
-            jax.ShapeDtypeStruct((ROWS, feats), bf16),
-            jax.ShapeDtypeStruct((ROWS, feats), bf16),
+            jax.ShapeDtypeStruct((ROWS, 2 * feats), bf16),
             jax.ShapeDtypeStruct((SPLIT - ROWS, width), f32),
             jax.ShapeDtypeStruct((10, SPLIT - ROWS, LANES), f32),
             jax.ShapeDtypeStruct((12,), jnp.int32),
@@ -337,18 +352,16 @@
             pltpu.VMEM((width, 3 * feats), bf16),
             pltpu.VMEM((feats, width), bf16),
             pltpu.VMEM((count, width), bf16),
-            pltpu.VMEM((count, feats), bf16),
-            pltpu.VMEM((count, feats), bf16),
-            pltpu.VMEM((count, feats), bf16),
-            pltpu.VMEM((ROWS, feats), bf16),
-            pltpu.VMEM((ROWS, width), f32),
+            pltpu.VMEM((count, 3 * feats), bf16),
+            pltpu.VMEM((count - ROWS, feats), bf16),
+            pltpu.VMEM((count - ROWS, width), f32),
             pltpu.VMEM((count, width), f32),
             pltpu.VMEM((10, HALO + count, LANES), f32),
             pltpu.VMEM((late, width), bf16),
             pltpu.VMEM((9, late // 32 + 8, 8, LANES), f32),
             pltpu.VMEM((9, late // 32 + 1, 8, LANES), f32),
             pltpu.VMEM((late, LANES), f32),
-            pltpu.SemaphoreType.DMA((5,)),
+            pltpu.SemaphoreType.DMA((8,)),
             pltpu.SemaphoreType.DMA((10,)),
         ],
         compiler_params=pltpu.CompilerParams(vmem_limit_bytes=56 << 20),
@@ -357,10 +370,10 @@
     )(segs, place, x, w_query, w_key, w_value, w_out, ln_gain, conv_gain, conv_weight)
     out = pl.pallas_call(
         kernel_b,
-        in_specs=[smem] + [hbm] * 6 + [vmem] * 3 + [hbm] * 6,
+        in_specs=[smem, hbm, pl.BlockSpec(memory_space=pltpu.HBM)] + [hbm] * 4 + [vmem] * 3 + [hbm] * 5,
         out_specs=hbm,
         out_shape=jax.ShapeDtypeStruct((count, width), bf16),
-        input_output_aliases={15: 0},
+        input_output_aliases={14: 0},
         scratch_shapes=[
             pltpu.VMEM((EXTRA, width), bf16),
             pltpu.VMEM((ROWS, width), bf16),
@@ -368,8 +381,7 @@
             pltpu.VMEM((feats, width), bf16),
             pltpu.VMEM((EXTRA, width), bf16),
             pltpu.VMEM((EXTRA, feats), bf16),
-            pltpu.VMEM((EXTRA + ROWS, feats), bf16),
-            pltpu.VMEM((EXTRA + ROWS, feats), bf16),
+            pltpu.VMEM((EXTRA + ROWS, 2 * feats), bf16),
             pltpu.VMEM((EXTRA, feats), bf16),
             pltpu.VMEM((EXTRA, width), f32),
             pltpu.VMEM((SPLIT, width), f32),
@@ -379,13 +391,13 @@
             pltpu.VMEM((9, SPLIT // 32 + 8, 8, LANES), f32),
             pltpu.VMEM((9, SPLIT // 32 + 1, 8, LANES), f32),
             pltpu.VMEM((SPLIT, LANES), f32),
-            pltpu.SemaphoreType.DMA((11,)),
+            pltpu.SemaphoreType.DMA((10,)),
             pltpu.SemaphoreType.DMA((10,)),
         ],
         compiler_params=pltpu.CompilerParams(vmem_limit_bytes=56 << 20),
         cost_estimate=pl.CostEstimate(flops=4_000_000_000, bytes_accessed=9_000_000, transcendentals=1_000_000),
         name="first_rows",
-    )(flags, x, tail, w_query, w_key, w_value, w_out, ln_gain, conv_gain, conv_weight, q0, k0, v0, hid0, cin0, out)
+    )(flags, x, tail, w_query, w_key, w_value, w_out, ln_gain, conv_gain, conv_weight, q0, kv0, hid0, cin0, out)
     return out[None]
 
 

time: 47.9 us -> 44.7 us (0.933)
  Pallas kernels: 38.8 us -> 37.2 us
  local copies, waits for them, and re-layouts: 3.57 us -> 2.03 us
    pallas_call x1, Pallas kernels: 24.5 us -> 23.4 us  [per_device(): pl.pallas_call(kernel_a, in_specs=[smem, smem, hbm, hbm, hbm, hbm, hbm, v...]
    unnamed x3 -> x2, local copies, waits for them, and re-layouts: 1.67 us -> 0.86 us
    reshape x1 -> x0, local copies, waits for them, and re-layouts: 0.74 us -> none  [per_device(): segs = segments.reshape(2 * SEGS)]
  transfers between devices with their start and end apart: 1 -> 1, of which waited for: 0 -> 0; matrix products, arithmetic and copies ran while one was open for 3% -> 0% of each run, Pallas kernels for 52% -> 53%
where the time goes in v3:
time: 44.7 us; the launch traced here: 43.9 us
  Pallas kernels  37.2 us (83%)
  starting transfers between devices  4.42 us (10%)
  local copies, waits for them, and re-layouts  2.03 us (5%)
    pallas_call x1, Pallas kernels, per_device(): pl.pallas_call(kernel_a, in_specs=[smem, smem, hbm, hbm, hbm, hbm, hbm, v...  23.4 us
    pallas_call x1, Pallas kernels, per_device(): pl.pallas_call(kernel_b, in_specs=[smem, hbm, pl.BlockSpec(memory_space=p...  13.9 us
    ppermute x1, starting transfers between devices, per_device(): lax.ppermute(x[count - EXTRA:], 'tm', [(i, i + 1) for i in range(peers -...  4.42 us
    slice x1, local copies, waits for them, and re-layouts, per_device(): x[count - EXTRA:]  1.16 us
  transfers between devices with their start and end apart: 1, of which 0 were waited for; matrix products, arithmetic and copies ran while one was open for 0% of the time, Pallas kernels for 53%

profile of v3, /device:TPU:1, one launch (start us, length us, event | category | flops | bytes accessed | tf_op | source)
XLA Modules:
  0.0 43.9 jit_solution(10760412522005106277)
XLA Ops:
  0.0 1.2 %slice_bitcast_fusion = bf16[288,1280]{1,0:T(8,128)(2,1)S(1)} fusion(bf16[1,1024,1280]{2,1,0:T(8,128)(2,1)} %param.9), kind=kLoop, calls=%fused_computation | loop fusion | bytes 1474560 | tf_op jit(solution)/shard_map/slice | solution.py:330
  1.2 4.4 %collective-permute-start = (bf16[288,1280]{1,0:T(8,128)(2,1)S(1)}, bf16[288,1280]{1,0:T(8,128)(2,1)S(1)}, u32[]{:S(2)}, u32[]{:S(2)}) collective-permute-start(bf16[288,1280]{1,0:T(8,128)(2,1)S(1)} %slice_bitcast_fusion), channel_id=1, source_target_pairs={{0,1},{1,2},{2,3},{3,4},{4,5},{5,6},{6,7},{7,8},{8,9},{9,10},{10,1... | collective-permute-start | bytes 2211848 | tf_op jit(solution)/shard_map/ppermute | solution.py:330
  5.6 23.4 %own_rows.1 = (bf16[1024,1280]{1,0:T(8,128)(2,1)}, bf16[256,640]{1,0:T(8,128)(2,1)}, bf16[256,1280]{1,0:T(8,128)(2,1)}, f32[224,1280]{1,0:T(8,128)}, f32[10,224,128]{2,1,0:T(8,128)}, /*index=5*/s32[12]{0:T(128)}) custom-call(s32[2,256]{1,0:T(2,128)} %bitcast.10, s32[1]{0:T(128)} %bitcast.2.place, bf16[1024,1280]{1,0:T(8,128)(2,1)} %bitcast.8, ...), custom_call_target="tpu_custom_call" | custom-call | flops 12000000000 | bytes 11000000 | tf_op jit(solution)/shard_map/own_rows/pallas_call | solution.py:338
  29.0 0.0 collective-permute-done.tail_hbm
  29.0 0.0 copy-start
  29.0 0.9 %copy-done = bf16[288,1280]{1,0:T(8,128)(2,1)} copy-done((bf16[288,1280]{1,0:T(8,128)(2,1)}, bf16[288,1280]{1,0:T(8,128)(2,1)S(1)}, u32[]{:S(2)}) %copy-start) | copy-done | bytes 737304
  29.8 13.9 %first_rows.1 = bf16[1024,1280]{1,0:T(8,128)(2,1)} custom-call(s32[12]{0:T(128)} %get-tuple-element.11.flags, bf16[1024,1280]{1,0:T(8,128)(2,1)} %bitcast.9, bf16[288,1280]{1,0:T(8,128)(2,1)} %copy-done, bf16[1280,640]{1,0:T(8,128)(2,1)} %wq_hbm.3, bf16[1280,640]{1,0:T(8,128)(2,1)} %wk_hbm.3, ...), custom_call_target="tpu_custom_call", output_to_operand_aliasing={{}: (14, {})} | custom-call | flops 4000000000 | bytes 9000000 | tf_op jit(solution)/shard_map/first_rows/pallas_call | solution.py:371
Async XLA Ops:
  1.2 27.8 %collective-permute-start = (bf16[288,1280]{1,0:T(8,128)(2,1)S(1)}, bf16[288,1280]{1,0:T(8,128)(2,1)S(1)}, u32[]{:S(2)}, u32[]{:S(2)}) collective-permute-start(bf16[288,1280]{1,0:T(8,128)(2,1)S(1)} %slice_bitcast_fusion), channel_id=1, source_target_pairs={{0,1},{1,2},{2,3},{3,4},{4,5},{5,6},{6,7},{7,8},{8,9},{9,10},{10,1... | collective-permute-start | bytes 2211848 | tf_op jit(solution)/shard_map/ppermute | solution.py:330
  29.0 0.9 %copy-start = (bf16[288,1280]{1,0:T(8,128)(2,1)}, bf16[288,1280]{1,0:T(8,128)(2,1)S(1)}, u32[]{:S(2)}) copy-start(bf16[288,1280]{1,0:T(8,128)(2,1)S(1)} %collective-permute-done.tail_hbm) | copy-start | bytes 2211844

commit v4 on v3

--- a/solution.py
+++ b/solution.py
@@ -63,10 +63,15 @@
 
 def attend(q_ref, q_first, k_ref, v_ref, prev_first, rows, bias, tri, heads_ref, out_first):
     cur_first = prev_first + ROWS
+    stack = rows < ROWS
     lane = lax.broadcasted_iota(jnp.int32, (rows, LANES), 1)
+    if stack:
+        tri = jnp.concatenate([tri, tri], axis=0)
+        bias = jnp.concatenate([bias, bias], axis=0)
     tri01 = jnp.where(tri, 1.0, 0.0).astype(jnp.bfloat16)
     ones = jnp.ones((ROWS, LANES), jnp.bfloat16)
     zero = jnp.zeros((rows, LANES), jnp.bfloat16)
+    dims = (((1,), (1,)), ((), ()))
     for pair in range(H // 2):
         cols = slice(pair * LANES, (pair + 1) * LANES)
         q = q_ref[pl.ds(q_first, rows), cols]
@@ -74,11 +79,11 @@
         kc = k_ref[pl.ds(cur_first, ROWS), cols]
         vp = jnp.concatenate([v_ref[pl.ds(prev_first, ROWS), cols], ones], axis=1)
         vc = jnp.concatenate([v_ref[pl.ds(cur_first, ROWS), cols], ones], axis=1)
+        halves = [jnp.where(lane < HS, q, zero), jnp.where(lane >= HS, q, zero)]
+        if stack:
+            halves = [jnp.concatenate(halves, axis=0)]
         outs = []
-        for half in range(2):
-            mine = (lane < HS) if half == 0 else (lane >= HS)
-            qh = jnp.where(mine, q, zero)
-            dims = (((1,), (1,)), ((), ()))
+        for qh in halves:
             sp = lax.dot_general(qh, kp, dims, preferred_element_type=jnp.float32)
             sc = lax.dot_general(qh, kc, dims, preferred_element_type=jnp.float32)
             s = jnp.where(tri, sc, sp) + bias
@@ -90,34 +95,42 @@
                 jnp.dot(pp, vp, preferred_element_type=jnp.float32)
                 + jnp.dot(pc, vc, preferred_element_type=jnp.float32)
             )
+        if stack:
+            outs = [outs[0][:rows], outs[0][rows:]]
         first = lane < HS
         num = jnp.where(first, outs[0][:, :LANES], outs[1][:, :LANES])
         den = jnp.where(first, outs[0][:, LANES:], outs[1][:, LANES:])
         heads_ref[pl.ds(out_first, rows), cols] = (num / den).astype(jnp.bfloat16)
 
 
-def fir_weights(w_ref, cols):
+def fill_weights(w_ref, table):
     def add(a, b):
         return a if b is None else a + b
 
-    w = [w_ref[pl.ds(j, 1), cols] for j in range(KSZ)] + [None]
+    w = [w_ref[pl.ds(j, 1), :] * 0.5 for j in range(KSZ)] + [None]
     even, odd = w[0::2], w[1::2]
     sets = []
     for h in (even, odd, [add(a, b) for a, b in zip(even, odd)]):
         first, second = h[0::2], h[1::2]
         sets += [first, second, [add(a, b) for a, b in zip(first, second)]]
-    return [[None if t is None else jnp.broadcast_to(t, (8, LANES)) for t in h] for h in sets]
+    for f, h in enumerate(sets):
+        for m, t in enumerate(h):
+            table[pl.ds(8 * f + m, 1), :] = jnp.zeros_like(w[0]) if t is None else t
 
 
 def conv_seg(cbuf, w_ref, c, cols, base, units, comb, part, ybuf):
     seg = 4 * units
-    weights = fir_weights(w_ref, cols)
+    zero_tap = (4, 7)
     for u in range(-8, units):
         x = [cbuf[c, pl.ds(base + HALO + 4 * u + p, 8, stride=seg), :] for p in range(4)]
         low, high = x[0] + x[1], x[2] + x[3]
         for f, t in enumerate((x[0], x[2], x[0] + x[2], x[1], x[3], x[1] + x[3], low, high, low + high)):
             comb[f, u + 8] = t
-    for f, h in enumerate(weights):
+    for f in range(9):
+        h = [
+            None if (f, m) == zero_tap else jnp.broadcast_to(w_ref[pl.ds(8 * f + m, 1), cols], (8, LANES))
+            for m in range(8)
+        ]
         lo = 0 if f in (0, 2, 6, 8) else -1
         xs = {u: comb[f, u + 8] for u in range(lo - 7, units)}
         for u in range(lo, units):
@@ -168,7 +181,7 @@
         conv_seg(cbuf, w_ref, c, cols, first, units, comb, part, ybuf)
         for r in range(0, count, 32):
             on = flags[3 + (first + r) // LANES] > 0
-            half = ybuf[pl.ds(r, 32), :] * 0.5
+            half = ybuf[pl.ds(r, 32), :]
             hidden = hid_ref[pl.ds(first + r, 32), cols]
             out = jnp.where(on, hidden + (half + half * jnp.tanh(half)), hidden)
             out_ref[pl.ds(r, 32), cols] = out.astype(jnp.bfloat16)
@@ -202,7 +215,7 @@
 
 
 def kernel_a(segs, place, x_hbm, wq_hbm, wk_hbm, wv_hbm, wo_hbm, g1, g2, cw, out_hbm, q0, kv0, hid0, cin0, flags0,
-             x, wqkv, wo, normed, qkv, heads, attn, hid, cbuf, out, comb, part, ybuf, sems, out_sems):
+             x, wqkv, wo, normed, qkv, heads, attn, hid, cbuf, out, comb, part, ybuf, sems, out_sems, table):
     feats = H * HS
     q, k, v = (qkv.at[:, pl.ds(i * feats, feats)] for i in range(3))
     copies = [
@@ -220,6 +233,7 @@
     for i in range(11):
         flags0[i] = flags[i]
     flags0[11] = jnp.minimum(place[0], 1)
+    fill_weights(cw, table)
     gain1 = g1[...].reshape(1, -1)
     gain2 = g2[...].reshape(1, -1)
     def project(b, lo, hi):
@@ -264,13 +278,13 @@
     ]
     for copy in rest:
         copy.start()
-    conv_rows(cbuf, cw, hid, flags, SPLIT, (1024 - SPLIT) // 32, comb, part, ybuf, out, out_hbm, out_sems)
+    conv_rows(cbuf, table, hid, flags, SPLIT, (1024 - SPLIT) // 32, comb, part, ybuf, out, out_hbm, out_sems)
     for copy in first + rest:
         copy.wait()
 
 
 def kernel_b(flags, x_hbm, tail_hbm, wq_hbm, wk_hbm, wv_hbm, wo_hbm, g1, g2, cw, q0, kv0, hid0, cin0, _, out_hbm,
-             tail, x, wqkv, wo, normed, q, kv, heads, attn, hid, halo_hid, cbuf, out, comb, part, ybuf, sems, out_sems):
+             tail, x, wqkv, wo, normed, q, kv, heads, attn, hid, halo_hid, cbuf, out, comb, part, ybuf, sems, out_sems, table):
     feats = H * HS
     k, v = (kv.at[:, pl.ds(i * feats, feats)] for i in range(2))
     copies = [
@@ -287,6 +301,7 @@
     ]
     for copy in copies:
         copy.start()
+    fill_weights(cw, table)
     gain1 = g1[...].reshape(1, -1)
     gain2 = g2[...].reshape(1, -1)
     copies[0].wait()
@@ -318,7 +333,7 @@
     keep = jnp.where(flags[11] > 0, 1.0, 0.0)
     residual(tail, CTX, attn, flags, [(HALO, 2)], halo_hid, 0, cbuf, 0, gain2, keep)
     residual(x, 0, attn.at[pl.ds(HALO, ROWS), :], flags, [(128, 3), (256, 4)], hid, 0, cbuf, HALO, gain2)
-    conv_rows(cbuf, cw, hid, flags, 0, SPLIT // 32, comb, part, ybuf, out, out_hbm, out_sems)
+    conv_rows(cbuf, table, hid, flags, 0, SPLIT // 32, comb, part, ybuf, out, out_hbm, out_sems)
 
 
 def per_device(frames, segments, ln_gain, w_query, w_key, w_value, w_out, conv_gain, conv_weight):
@@ -363,8 +378,9 @@
             pltpu.VMEM((late, LANES), f32),
             pltpu.SemaphoreType.DMA((8,)),
             pltpu.SemaphoreType.DMA((10,)),
+            pltpu.VMEM((72, width), f32),
         ],
-        compiler_params=pltpu.CompilerParams(vmem_limit_bytes=56 << 20),
+        compiler_params=pltpu.CompilerParams(vmem_limit_bytes=63 << 20),
         cost_estimate=pl.CostEstimate(flops=12_000_000_000, bytes_accessed=11_000_000, transcendentals=4_000_000),
         name="own_rows",
     )(segs, place, x, w_query, w_key, w_value, w_out, ln_gain, conv_gain, conv_weight)
@@ -393,8 +409,9 @@
             pltpu.VMEM((SPLIT, LANES), f32),
             pltpu.SemaphoreType.DMA((10,)),
             pltpu.SemaphoreType.DMA((10,)),
+            pltpu.VMEM((72, width), f32),
         ],
-        compiler_params=pltpu.CompilerParams(vmem_limit_bytes=56 << 20),
+        compiler_params=pltpu.CompilerParams(vmem_limit_bytes=63 << 20),
         cost_estimate=pl.CostEstimate(flops=4_000_000_000, bytes_accessed=9_000_000, transcendentals=1_000_000),
         name="first_rows",
     )(flags, x, tail, w_query, w_key, w_value, w_out, ln_gain, conv_gain, conv_weight, q0, kv0, hid0, cin0, out)

time: 44.7 us -> 43.4 us (0.971); the launches traced: 43.9 us -> 43.2 us
  local copies, waits for them, and re-layouts: 2.03 us -> 1.16 us
  starting transfers between devices: 4.42 us -> 5.25 us
  Pallas kernels: 37.2 us -> 36.6 us
    unnamed x2 -> x0, local copies, waits for them, and re-layouts: 0.86 us -> none
    ppermute x1, starting transfers between devices: 4.42 us -> 5.25 us  [per_device(): lax.ppermute(x[count - EXTRA:], 'tm', [(i, i + 1) for i in range(peers -...]
    pallas_call x1, Pallas kernels: 13.9 us -> 13.4 us  [per_device(): pl.pallas_call(kernel_b, in_specs=[smem, hbm, pl.BlockSpec(memory_space=p...]
  transfers between devices with their start and end apart: 1 -> 1, of which waited for: 0 -> 0; matrix products, arithmetic and copies ran while one was open for 0% -> 0% of each run, Pallas kernels for 53% -> 54%
where the time goes in v4:
time: 43.4 us; the launch traced here: 43.2 us
  Pallas kernels  36.6 us (84%)
  starting transfers between devices  5.25 us (12%)
  local copies, waits for them, and re-layouts  1.16 us (3%)
    pallas_call x1, Pallas kernels, per_device(): pl.pallas_call(kernel_a, in_specs=[smem, smem, hbm, hbm, hbm, hbm, hbm, v...  23.3 us
    pallas_call x1, Pallas kernels, per_device(): pl.pallas_call(kernel_b, in_specs=[smem, hbm, pl.BlockSpec(memory_space=p...  13.4 us
    ppermute x1, starting transfers between devices, per_device(): lax.ppermute(x[count - EXTRA:], 'tm', [(i, i + 1) for i in range(peers -...  5.25 us
    slice x1, local copies, waits for them, and re-layouts, per_device(): x[count - EXTRA:]  1.16 us
  transfers between devices with their start and end apart: 1, of which 0 were waited for; matrix products, arithmetic and copies ran while one was open for 0% of the time, Pallas kernels for 54%

profile of v4, /device:TPU:1, one launch (start us, length us, event | category | flops | bytes accessed | tf_op | source)
XLA Modules:
  0.0 43.2 jit_solution(3156507267057441898)
XLA Ops:
  0.0 1.2 %slice_bitcast_fusion = bf16[288,1280]{1,0:T(8,128)(2,1)S(1)} fusion(bf16[1,1024,1280]{2,1,0:T(8,128)(2,1)} %param.9), kind=kLoop, calls=%fused_computation | loop fusion | bytes 1474560 | tf_op jit(solution)/shard_map/slice | solution.py:345
  1.2 5.2 %collective-permute-start = (bf16[288,1280]{1,0:T(8,128)(2,1)S(1)}, bf16[288,1280]{1,0:T(8,128)(2,1)}, u32[]{:S(2)}, u32[]{:S(2)}) collective-permute-start(bf16[288,1280]{1,0:T(8,128)(2,1)S(1)} %slice_bitcast_fusion), channel_id=1, source_target_pairs={{0,1},{1,2},{2,3},{3,4},{4,5},{5,6},{6,7},{7,8},{8,9},{9,10},{10,1... | collective-permute-start | bytes 2211848 | tf_op jit(solution)/shard_map/ppermute | solution.py:345
  6.4 23.3 %own_rows.1 = (bf16[1024,1280]{1,0:T(8,128)(2,1)}, bf16[256,640]{1,0:T(8,128)(2,1)}, bf16[256,1280]{1,0:T(8,128)(2,1)}, f32[224,1280]{1,0:T(8,128)}, f32[10,224,128]{2,1,0:T(8,128)}, /*index=5*/s32[12]{0:T(128)}) custom-call(s32[2,256]{1,0:T(2,128)} %bitcast.10, s32[1]{0:T(128)} %bitcast.2.place, bf16[1024,1280]{1,0:T(8,128)(2,1)} %bitcast.8, ...), custom_call_target="tpu_custom_call" | custom-call | flops 12000000000 | bytes 11000000 | tf_op jit(solution)/shard_map/own_rows/pallas_call | solution.py:353
  29.7 0.0 collective-permute-done.tail_hbm
  29.7 13.4 %first_rows.1 = bf16[1024,1280]{1,0:T(8,128)(2,1)} custom-call(s32[12]{0:T(128)} %get-tuple-element.11.flags, bf16[1024,1280]{1,0:T(8,128)(2,1)} %bitcast.9, bf16[288,1280]{1,0:T(8,128)(2,1)} %collective-permute-done.tail_hbm, bf16[1280,640]{1,0:T(8,128)(2,1)} %wq_hbm.3, bf16[1280,640]{1,0:T(8,128)(2,1)} %wk_hbm.3, ...), custom_call_target="tpu_custom_call", output_to_operand_aliasing={{}: (14, {})} | custom-call | flops 4000000000 | bytes 9000000 | tf_op jit(solution)/shard_map/first_rows/pallas_call | solution.py:387
Async XLA Ops:
  1.2 28.5 %collective-permute-start = (bf16[288,1280]{1,0:T(8,128)(2,1)S(1)}, bf16[288,1280]{1,0:T(8,128)(2,1)}, u32[]{:S(2)}, u32[]{:S(2)}) collective-permute-start(bf16[288,1280]{1,0:T(8,128)(2,1)S(1)} %slice_bitcast_fusion), channel_id=1, source_target_pairs={{0,1},{1,2},{2,3},{3,4},{4,5},{5,6},{6,7},{7,8},{8,9},{9,10},{10,1... | collective-permute-start | bytes 2211848 | tf_op jit(solution)/shard_map/ppermute | solution.py:345

commit v5 on v4

--- a/solution.py
+++ b/solution.py
@@ -176,7 +176,7 @@
 def conv_rows(cbuf, w_ref, hid_ref, flags, first, units, comb, part, ybuf, out_ref, out_hbm, sems):
     count = 32 * units
 
-    def lanes(c, carry):
+    def lanes(c, comb, part, ybuf):
         cols = pl.ds(pl.multiple_of(c * LANES, LANES), LANES)
         conv_seg(cbuf, w_ref, c, cols, first, units, comb, part, ybuf)
         for r in range(0, count, 32):
@@ -186,6 +186,10 @@
             out = jnp.where(on, hidden + (half + half * jnp.tanh(half)), hidden)
             out_ref[pl.ds(r, 32), cols] = out.astype(jnp.bfloat16)
         send(c).start()
+
+    def two(i, carry):
+        for j in range(2):
+            lanes(2 * i + j, comb.at[j], part.at[j], ybuf.at[j])
         return carry
 
     def send(c):
@@ -198,7 +202,7 @@
         send(c).wait()
         return carry
 
-    lax.fori_loop(0, 10, lanes, 0)
+    lax.fori_loop(0, 5, two, 0)
     lax.fori_loop(0, 10, finish, 0)
 
 
@@ -373,9 +377,9 @@
             pltpu.VMEM((count, width), f32),
             pltpu.VMEM((10, HALO + count, LANES), f32),
             pltpu.VMEM((late, width), bf16),
-            pltpu.VMEM((9, late // 32 + 8, 8, LANES), f32),
-            pltpu.VMEM((9, late // 32 + 1, 8, LANES), f32),
-            pltpu.VMEM((late, LANES), f32),
+            pltpu.VMEM((2, 9, late // 32 + 8, 8, LANES), f32),
+            pltpu.VMEM((2, 9, late // 32 + 1, 8, LANES), f32),
+            pltpu.VMEM((2, late, LANES), f32),
             pltpu.SemaphoreType.DMA((8,)),
             pltpu.SemaphoreType.DMA((10,)),
             pltpu.VMEM((72, width), f32),
@@ -404,9 +408,9 @@
             pltpu.VMEM((HALO, width), f32),
             pltpu.VMEM((10, HALO + SPLIT, LANES), f32),
             pltpu.VMEM((SPLIT, width), bf16),
-            pltpu.VMEM((9, SPLIT // 32 + 8, 8, LANES), f32),
-            pltpu.VMEM((9, SPLIT // 32 + 1, 8, LANES), f32),
-            pltpu.VMEM((SPLIT, LANES), f32),
+            pltpu.VMEM((2, 9, SPLIT // 32 + 8, 8, LANES), f32),
+            pltpu.VMEM((2, 9, SPLIT // 32 + 1, 8, LANES), f32),
+            pltpu.VMEM((2, SPLIT, LANES), f32),
             pltpu.SemaphoreType.DMA((10,)),
             pltpu.SemaphoreType.DMA((10,)),
             pltpu.VMEM((72, width), f32),

time: 43.4 us -> 43.1 us (level)
  no operation moved by 1% of the time
where the time goes in v5:
time: 43.1 us; the launch traced here: 43 us
  Pallas kernels  36.4 us (84%)
  starting transfers between devices  5.25 us (12%)
  local copies, waits for them, and re-layouts  1.16 us (3%)
    pallas_call x1, Pallas kernels, per_device(): pl.pallas_call(kernel_a, in_specs=[smem, smem, hbm, hbm, hbm, hbm, hbm, v...  23.1 us
    pallas_call x1, Pallas kernels, per_device(): pl.pallas_call(kernel_b, in_specs=[smem, hbm, pl.BlockSpec(memory_space=p...  13.3 us
    ppermute x1, starting transfers between devices, per_device(): lax.ppermute(x[count - EXTRA:], 'tm', [(i, i + 1) for i in range(peers -...  5.25 us
    slice x1, local copies, waits for them, and re-layouts, per_device(): x[count - EXTRA:]  1.16 us
  transfers between devices with their start and end apart: 1, of which 0 were waited for; matrix products, arithmetic and copies ran while one was open for 0% of the time, Pallas kernels for 54%

profile of v5, /device:TPU:1, one launch (start us, length us, event | category | flops | bytes accessed | tf_op | source)
XLA Modules:
  0.0 43.0 jit_solution(2264493174835873882)
XLA Ops:
  0.0 1.2 %slice_bitcast_fusion = bf16[288,1280]{1,0:T(8,128)(2,1)S(1)} fusion(bf16[1,1024,1280]{2,1,0:T(8,128)(2,1)} %param.9), kind=kLoop, calls=%fused_computation | loop fusion | bytes 1474560 | tf_op jit(solution)/shard_map/slice | solution.py:349
  1.2 5.2 %collective-permute-start = (bf16[288,1280]{1,0:T(8,128)(2,1)S(1)}, bf16[288,1280]{1,0:T(8,128)(2,1)}, u32[]{:S(2)}, u32[]{:S(2)}) collective-permute-start(bf16[288,1280]{1,0:T(8,128)(2,1)S(1)} %slice_bitcast_fusion), channel_id=1, source_target_pairs={{0,1},{1,2},{2,3},{3,4},{4,5},{5,6},{6,7},{7,8},{8,9},{9,10},{10,1... | collective-permute-start | bytes 2211848 | tf_op jit(solution)/shard_map/ppermute | solution.py:349
  6.4 23.1 %own_rows.1 = (bf16[1024,1280]{1,0:T(8,128)(2,1)}, bf16[256,640]{1,0:T(8,128)(2,1)}, bf16[256,1280]{1,0:T(8,128)(2,1)}, f32[224,1280]{1,0:T(8,128)}, f32[10,224,128]{2,1,0:T(8,128)}, /*index=5*/s32[12]{0:T(128)}) custom-call(s32[2,256]{1,0:T(2,128)} %bitcast.10, s32[1]{0:T(128)} %bitcast.2.place, bf16[1024,1280]{1,0:T(8,128)(2,1)} %bitcast.8, ...), custom_call_target="tpu_custom_call" | custom-call | flops 12000000000 | bytes 11000000 | tf_op jit(solution)/shard_map/own_rows/pallas_call | solution.py:357
  29.5 0.0 collective-permute-done.tail_hbm
  29.5 13.3 %first_rows.1 = bf16[1024,1280]{1,0:T(8,128)(2,1)} custom-call(s32[12]{0:T(128)} %get-tuple-element.11.flags, bf16[1024,1280]{1,0:T(8,128)(2,1)} %bitcast.9, bf16[288,1280]{1,0:T(8,128)(2,1)} %collective-permute-done.tail_hbm, bf16[1280,640]{1,0:T(8,128)(2,1)} %wq_hbm.3, bf16[1280,640]{1,0:T(8,128)(2,1)} %wk_hbm.3, ...), custom_call_target="tpu_custom_call", output_to_operand_aliasing={{}: (14, {})} | custom-call | flops 4000000000 | bytes 9000000 | tf_op jit(solution)/shard_map/first_rows/pallas_call | solution.py:391
Async XLA Ops:
  1.2 28.4 %collective-permute-start = (bf16[288,1280]{1,0:T(8,128)(2,1)S(1)}, bf16[288,1280]{1,0:T(8,128)(2,1)}, u32[]{:S(2)}, u32[]{:S(2)}) collective-permute-start(bf16[288,1280]{1,0:T(8,128)(2,1)S(1)} %slice_bitcast_fusion), channel_id=1, source_target_pairs={{0,1},{1,2},{2,3},{3,4},{4,5},{5,6},{6,7},{7,8},{8,9},{9,10},{10,1... | collective-permute-start | bytes 2211848 | tf_op jit(solution)/shard_map/ppermute | solution.py:349
